TPU v7x, 256 devices: a whole 4x4x8 slice. The times are simulated.
256 devices in a mesh: comp: 2 (over core), lat: 16 (over z_hi, y), lon: 8 (over x, z_lo).
Axes of the slice: x: 4, y: 4, z: 8 (z_hi: 4, z_lo: 2; z = z_hi * 2 + z_lo), core: 2. Of those that a mesh axis runs over, the one named last changes fastest.
Arguments:
- state: bfloat16 [2, 256, 1024, 384], P('comp', 'lat', 'lon'), may hold values from -6 to 6
- source_cell: int32 [2, 4, 256, 1024], P('comp', None, 'lat', 'lon'), may hold values from 0 to 262143, as said below
- remap_weight: float32 [2, 4, 256, 1024], P('comp', None, 'lat', 'lon'), may hold values from 0.1 to 1
- sea_mask: int32 [2, 256, 1024], P('comp', 'lat', 'lon'), may hold values 0 or 1
- spectral_weight: bfloat16 [2, 384, 384], P('comp'), may hold values from -0.3125 to 0.3125
- cotangent: bfloat16 [2, 256, 1024, 384], P('comp', 'lat', 'lon'), may hold values from -6 to 6
Outputs:
- updated: bfloat16 [2, 256, 1024, 384], P('comp', 'lat', 'lon')
- weight_grad: float32 [2, 384, 384], P('comp')
Inputs may be any that keep to these rules, and one draw needn't show every extreme that they name: `source_cell`: A cell index row * 1024 + longitude of the other component's grid; its row differs from the target cell's row by at most 8, and its longitude lies in the same aligned block of 128 longitudes as the target's.
All inputs are finite; a program needn't handle non-finite values. No bound on the sum of `sea_mask` on one device may be relied on, other than what follows from the above.
Results may differ from a plain program's by a relative error of at most 0.0086.
Values may be sent and summed in bfloat16 or wider, within the bound.
No kernel may reach another device: no remote copies, remote signals or barrier semaphores. Data moves between devices by JAX's collectives and lax.ppermute only.
A program may use at most 64 MiB of HBM per device.

v0:
```python
import functools
import math

import jax
import jax.numpy as jnp
import ml_dtypes
import numpy as np
from jax import lax
from jax.experimental import pallas as pl
from jax.experimental.pallas import tpu as pltpu
from jax.sharding import PartitionSpec as P

M = 384
K = 4
REACH = 8
QUAD = 4
SPAN = 512
RING = 4
CLOSE = 5
NLON_BITS = 10
MIB = 1 << 20


def low_pass(nlon, modes):
    phase = (np.arange(nlon)[:, None] * np.arange(modes)[None, :]) % nlon
    angle = phase * (2.0 * math.pi / nlon)
    norm = 1.0 / math.sqrt(nlon)
    table = np.concatenate([np.cos(angle) * norm, -np.sin(angle) * norm], axis=1)
    table = table.astype(np.float32).astype(ml_dtypes.bfloat16).astype(np.float64)
    factor = np.where(np.arange(modes) == 0, 1.0, 2.0)
    factor = np.concatenate([factor, factor])
    return ((table * factor) @ table.T).astype(np.float32).astype(ml_dtypes.bfloat16)


def near_kernel(
    lat_ref, cell_ref, weight_ref, mask_ref, source_ref, own_ref,
    partial_ref, close_ref, far_ref, place_ref, merged_ref, near_ref,
):
    rows, lon_dev = mask_ref.shape
    first = lat_ref[0] * rows
    sea = mask_ref[...].astype(jnp.float32)
    for term in range(K):
        cell = cell_ref[term]
        place_ref[term] = (lax.shift_right_logical(cell, NLON_BITS) - first) * lon_dev + (
            cell & (lon_dev - 1)
        )
    for term in range(K):
        value = weight_ref[term]
        for other in range(term):
            value = value + jnp.where(place_ref[other] == place_ref[term], weight_ref[other], 0.0)
        merged_ref[term] = value * sea
    ids = lax.broadcasted_iota(jnp.int16, (lon_dev, lon_dev), 0)

    def lines(row):
        place = [place_ref[t, row : row + 1, :].astype(jnp.int16) for t in range(K)]
        share = [merged_ref[t, row : row + 1, :].astype(jnp.bfloat16) for t in range(K)]
        return place, share

    def tile(place, share, start):
        cells = ids + jnp.asarray(start * lon_dev, jnp.int32).astype(jnp.int16)
        out = jnp.zeros((lon_dev, lon_dev), jnp.bfloat16)
        for term in range(K):
            out = jnp.where(place[term] == cells, share[term], out)
        return out

    half = rows // 2
    for row in range(rows):
        place, share = lines(row)
        span = slice(row * lon_dev, (row + 1) * lon_dev)
        low, high = band(row // QUAD, rows)

        def build(source, _):
            at = pl.multiple_of(source * lon_dev, lon_dev)
            near_ref[pl.ds(at, lon_dev), span] = tile(place, share, source)
            return 0

        lax.fori_loop(low, high, build, 0)
        close_first = -CLOSE if row < half else rows

        def build_close(source, _):
            at = pl.multiple_of(source * lon_dev, lon_dev)
            close_ref[pl.ds(at, lon_dev), span] = tile(place, share, source + close_first)
            return 0

        lax.fori_loop(0, CLOSE, build_close, 0)
        if row < QUAD or row >= rows - QUAD:
            far_first = -REACH if row < half else rows + CLOSE
            place_at = row if row < half else row - rows + 2 * QUAD
            far_span = slice(place_at * lon_dev, (place_at + 1) * lon_dev)
            for source in range(REACH - CLOSE):
                far_ref[source * lon_dev : (source + 1) * lon_dev, far_span] = tile(
                    place, share, source + far_first
                )
    size = QUAD * lon_dev
    for block in range(rows // QUAD):
        low, high = band(block, rows)
        span = slice(block * size, (block + 1) * size)
        partial_ref[span, :] = own_ref[span, :].astype(jnp.float32) + across(
            near_ref[low * lon_dev : high * lon_dev, span],
            source_ref[low * lon_dev : high * lon_dev, :],
        )


def across(left, right):
    return lax.dot_general(
        left, right, (((0,), (0,)), ((), ())), preferred_element_type=jnp.float32
    )


def band(block, rows):
    return max(0, block * QUAD - REACH), min(rows, block * QUAD + QUAD + REACH)


def near_part(lat, cells, weight, mask, source, own):
    targets, channels = own.shape
    rows, lon_dev = mask.shape
    vmem = pl.BlockSpec(memory_space=pltpu.VMEM)
    return pl.pallas_call(
        near_kernel,
        out_shape=(
            jax.ShapeDtypeStruct((targets, channels), jnp.float32),
            jax.ShapeDtypeStruct((CLOSE * lon_dev, targets), jnp.bfloat16),
            jax.ShapeDtypeStruct(((REACH - CLOSE) * lon_dev, 2 * QUAD * lon_dev), jnp.bfloat16),
        ),
        in_specs=[pl.BlockSpec(memory_space=pltpu.SMEM)] + [vmem] * 5,
        out_specs=(vmem,) * 3,
        scratch_shapes=[
            pltpu.VMEM(cells.shape, jnp.int32),
            pltpu.VMEM(cells.shape, jnp.float32),
            pltpu.VMEM((targets, targets), jnp.bfloat16),
        ],
        compiler_params=pltpu.CompilerParams(vmem_limit_bytes=40 * MIB),
        cost_estimate=pl.CostEstimate(
            flops=2 * targets * targets * channels, bytes_accessed=16 * MIB, transcendentals=0
        ),
    )(lat, cells, weight, mask, source, own)


def edge_kernel(rows, close_ref, far_ref, partial_ref, low_close_ref, low_far_ref, high_close_ref, high_far_ref, forced_ref):
    lon_dev = low_close_ref.shape[0] // CLOSE
    size, steps = QUAD * lon_dev, rows // QUAD
    for block in range(steps):
        below = block < steps // 2
        place = block if below else steps - 1 - block
        skip = max(0, QUAD * place - (REACH - CLOSE)) * lon_dev
        used = slice(skip, None) if below else slice(0, CLOSE * lon_dev - skip)
        span = slice(block * size, (block + 1) * size)
        halo_ref = low_close_ref if below else high_close_ref
        value = partial_ref[span, :] + across(close_ref[used, span], halo_ref[used, :])
        if place == 0:
            distant_ref = low_far_ref if below else high_far_ref
            far_span = slice(0, size) if below else slice(size, 2 * size)
            value = value + across(far_ref[:, far_span], distant_ref[...])
        forced_ref[span, :] = value.astype(forced_ref.dtype)


def edge_part(close, far, partial, low_close, low_far, high_close, high_far, rows):
    targets, channels = partial.shape
    vmem = pl.BlockSpec(memory_space=pltpu.VMEM)
    return pl.pallas_call(
        functools.partial(edge_kernel, rows),
        out_shape=jax.ShapeDtypeStruct((targets, channels), jnp.bfloat16),
        in_specs=[vmem] * 7,
        out_specs=vmem,
        compiler_params=pltpu.CompilerParams(vmem_limit_bytes=24 * MIB),
        cost_estimate=pl.CostEstimate(
            flops=2 * targets * close.shape[0] * channels, bytes_accessed=10 * MIB, transcendentals=0
        ),
    )(close, far, partial, low_close, low_far, high_close, high_far)


def spectral_kernel(scale, filter_ref, x_ref, cot_ref, weight_ref, out_ref, grad_ref):
    lon_count, rows, lon_dev, channels = x_ref.shape
    weight = weight_ref[...]
    total = jnp.zeros((channels, channels), jnp.float32)
    for row in range(rows):
        x = x_ref[:, row].reshape(-1, channels)
        for first in range(0, lon_count, SPAN // lon_dev):
            blocks = slice(first, first + SPAN // lon_dev)
            part = slice(first * lon_dev, first * lon_dev + SPAN)
            smooth = jnp.dot(filter_ref[part, :], x, preferred_element_type=jnp.float32)
            smooth = smooth.astype(jnp.bfloat16)
            synth = jnp.dot(smooth, weight, preferred_element_type=jnp.float32)
            sigma = 0.5 + 0.5 * jnp.tanh(0.5 * synth)
            mine = x_ref[blocks, row].reshape(SPAN, channels).astype(jnp.float32)
            moved = (mine + synth * sigma).astype(out_ref.dtype)
            out_ref[blocks, row] = moved.reshape(-1, lon_dev, channels)
            cot = cot_ref[blocks, row].reshape(SPAN, channels).astype(jnp.float32)
            grad = (cot * sigma * (1.0 + synth * (1.0 - sigma))).astype(jnp.bfloat16)
            total = total + across(smooth, grad)
    grad_ref[...] = (total * scale).astype(grad_ref.dtype)


def spectral_part(table, x, cot, weight, scale):
    lon_count, rows, lon_dev, channels = x.shape
    nlon = lon_count * lon_dev
    vmem = pl.BlockSpec(memory_space=pltpu.VMEM)
    return pl.pallas_call(
        functools.partial(spectral_kernel, scale),
        out_shape=(
            jax.ShapeDtypeStruct(x.shape, jnp.bfloat16),
            jax.ShapeDtypeStruct((channels, channels), jnp.bfloat16),
        ),
        in_specs=[vmem] * 4,
        out_specs=(vmem, vmem),
        compiler_params=pltpu.CompilerParams(vmem_limit_bytes=32 * MIB),
        cost_estimate=pl.CostEstimate(
            flops=2 * rows * nlon * channels * (nlon + 2 * channels),
            bytes_accessed=8 * MIB,
            transcendentals=rows * nlon * channels,
        ),
    )(table, x, cot, weight)


def spread(block, axis):
    return lax.all_to_all(block, axis, split_axis=0, concat_axis=0, tiled=True)


def fold(piece, step, shift):
    pairs = []
    for place in range(lax.axis_size("lat")):
        at = place // step % RING
        to = (((at + shift) ^ 1) - shift) % RING
        pairs.append((place, place + (to - at) * step))
    other = lax.ppermute(piece, "lat", pairs)
    return (piece.astype(jnp.float32) + other.astype(jnp.float32)).astype(jnp.bfloat16)


def finish(updated, grad):
    rows, columns = grad.shape
    count = lax.axis_size("lon")
    pieces = spread(grad.reshape(count, -1, columns), "lon")
    updated, pieces = lax.optimization_barrier((updated, pieces))
    updated = spread(updated, "lon")
    piece = jnp.sum(pieces.astype(jnp.float32), axis=0).astype(jnp.bfloat16)
    piece = fold(fold(piece, 1, 0), 1, 1)
    piece = fold(fold(piece, RING, 0), RING, 1)
    updated, piece = lax.optimization_barrier((updated, piece))
    copies = jnp.broadcast_to(piece[None], (count, *piece.shape))
    total = spread(copies, "lon").reshape(rows, columns).astype(jnp.float32)
    updated = jnp.where(lax.axis_index("lat") < lax.axis_size("lat"), updated, 0)
    return updated, total


def route(pairs, lat_count, swap):
    return [
        (comp * lat_count + low, (comp ^ swap) * lat_count + high)
        for comp in range(2)
        for low, high in pairs
    ]


def send(block, pairs, swap):
    return lax.ppermute(block, ("comp", "lat"), route(pairs, lax.axis_size("lat"), swap))


def halos(own, ready):
    lat_dev, lat_count = own.shape[0], lax.axis_size("lat")
    up = [(low, low + 1) for low in range(lat_count - 1)]
    down = [(high, low) for low, high in up]
    low_close = send(own[lat_dev - CLOSE :], up, 1)
    high_close = send(own[:CLOSE], down, 1)
    own, ready = lax.optimization_barrier((own, ready))
    inner = [pair for pair in up if pair[1] % RING]
    rings = range(0, lat_count - RING, RING)
    first_up = [(ring + RING - 1, ring) for ring in rings]
    first_down = [(ring + RING, ring + 2 * RING - 1) for ring in rings]
    turn = lambda pairs: [(high, low) for low, high in pairs]
    mixed = lambda pairs, relay: route(pairs, lat_count, 1) + route(relay, lat_count, 0)
    axes = ("comp", "lat")
    far_up = lax.ppermute(own[lat_dev - REACH : lat_dev - CLOSE], axes, mixed(inner, first_up))
    far_down = lax.ppermute(own[CLOSE:REACH], axes, mixed(turn(inner), first_down))
    over_up = send(far_up, [(ring, ring + RING) for ring in rings], 1)
    over_down = send(far_down, [(ring + 2 * RING - 1, ring + RING - 1) for ring in rings], 1)
    place = lax.axis_index("lat") % RING
    low_far = jnp.where(place == 0, over_up, far_up)
    high_far = jnp.where(place == RING - 1, over_down, far_down)
    return low_close, low_far, high_close, high_far, ready


def local(state, source_cell, remap_weight, sea_mask, spectral_weight, cotangent):
    own = state[0]
    lat_dev, lon_dev, channels = own.shape
    lon_count = lax.axis_size("lon")
    nlon = lon_dev * lon_count
    nlat = lat_dev * lax.axis_size("lat")
    flat = lambda block: block.reshape(-1, channels)

    source = lax.ppermute(own, "comp", [(0, 1), (1, 0)])
    *edges, source = halos(own, source)
    cot = cotangent[0]
    cot = spread(cot, "lon").reshape(lon_count, -1, lon_dev, channels)

    lat = lax.axis_index("lat").astype(jnp.int32).reshape(1)
    partial, close, far = near_part(
        lat, source_cell[0], remap_weight[0], sea_mask[0], flat(source), flat(own)
    )
    forced = edge_part(close, far, partial, *[flat(edge) for edge in edges], lat_dev)
    forced = spread(forced.reshape(own.shape), "lon").reshape(cot.shape)
    table = jnp.asarray(low_pass(nlon, M))
    scale = 1.0 / math.sqrt(2 * M * nlat)
    updated, grad = spectral_part(table, forced, cot, spectral_weight[0], scale)
    updated, total = finish(updated.reshape(own.shape), grad)
    return (updated[None], total[None])


def solution(mesh):
    in_specs = (
        P("comp", "lat", "lon", None),
        P("comp", None, "lat", "lon"),
        P("comp", None, "lat", "lon"),
        P("comp", "lat", "lon"),
        P("comp", None, None),
        P("comp", "lat", "lon", None),
    )
    out_specs = (P("comp", "lat", "lon", None), P("comp", None, None))
    return jax.shard_map(local, mesh=mesh, in_specs=in_specs, out_specs=out_specs, check_vma=False)
```

profile of v0, /device:TPU:24, one launch (start us, length us, event | category | flops | bytes accessed | tf_op | source)
XLA Modules:
  0.0 140.3 jit_solution(13211923125734150149)
XLA Ops:
  0.6 0.1 collective-permute-start
  0.7 5.8 %all-to-all-start.1 = ((bf16[16,128,384]{2,1,0:T(8,128)(2,1)}), bf16[16,128,384]{2,1,0:T(8,128)(2,1)S(1)}, u32[]{:S(2)}, u32[]{:S(2)}) async-start(bf16[16,128,384]{2,1,0:T(8,128)(2,1)} %bitcast.41), calls=%async_computation.1 | async-start | bytes 3145728 | tf_op jit(solution)/shard_map/all_to_all | solution.py:216
  6.6 0.9 fusion
  7.5 3.2 %collective-permute-start.5 = (bf16[3,128,384]{2,1,0:T(8,128)(2,1)}, bf16[3,128,384]{2,1,0:T(8,128)(2,1)}, u32[]{:S(2)}, u32[]{:S(2)}) collective-permute-start(bf16[3,128,384]{2,1,0:T(8,128)(2,1)} %get-tuple-element.24), channel_id=1, source_target_pairs={{8,128},{16,136},{24,144},{40,160},{48,168},{56,176},{72,192},{80,... | collective-permute-start | bytes 884744 | tf_op jit(solution)/shard_map/ppermute | solution.py:272
  10.7 1.9 %collective-permute-start.2 = (bf16[3,128,384]{2,1,0:T(8,128)(2,1)}, bf16[3,128,384]{2,1,0:T(8,128)(2,1)S(1)}, u32[]{:S(2)}, u32[]{:S(2)}) collective-permute-start(bf16[3,128,384]{2,1,0:T(8,128)(2,1)} %get-tuple-element.25), channel_id=1, source_target_pairs={{0,136},{8,144},{16,152},{32,168},{40,176},{48,184},{64,200},{72,2... | collective-permute-start | bytes 884744 | tf_op jit(solution)/shard_map/ppermute | solution.py:271
  12.6 1.1 slice_bitcast_fusion
  13.6 3.6 %collective-permute-start.4 = (bf16[5,128,384]{2,1,0:T(8,128)(2,1)}, bf16[5,128,384]{2,1,0:T(8,128)(2,1)}, u32[]{:S(2)}, u32[]{:S(2)}) collective-permute-start(bf16[5,128,384]{2,1,0:T(8,128)(2,1)} %get-tuple-element.26), channel_id=1, source_target_pairs={{8,128},{16,136},{24,144},{32,152},{40,160},{48,168},{56,176},{64,... | collective-permute-start | bytes 1474568 | tf_op jit(solution)/shard_map/ppermute | solution.py:254
  17.3 4.9 %collective-permute-start.1 = (bf16[5,128,384]{2,1,0:T(8,128)(2,1)}, bf16[5,128,384]{2,1,0:T(8,128)(2,1)}, u32[]{:S(2)}, u32[]{:S(2)}) collective-permute-start(bf16[5,128,384]{2,1,0:T(8,128)(2,1)} %get-tuple-element.27), channel_id=1, source_target_pairs={{0,136},{8,144},{16,152},{24,160},{32,168},{40,176},{48,184},{56,1... | collective-permute-start | bytes 1474568 | tf_op jit(solution)/shard_map/ppermute | solution.py:254
  22.2 1.3 collective-permute-start.6
  23.5 0.7 collective-permute-start.3
  24.3 11.1 %shard_map.86 = (f32[2048,384]{1,0:T(8,128)S(1)}, bf16[640,2048]{1,0:T(8,128)(2,1)S(1)}, bf16[384,1024]{1,0:T(8,128)(2,1)S(1)}) custom-call(s32[1]{0:T(128)} %bitcast.lat_ref, s32[4,16,128]{2,1,0:T(8,128)S(1)} %bitcast.38, f32[4,16,128]{2,1,0:T(8,128)S(1)} %bitcast.39, s32[16,128]{1,0:T(8,128)S(1)} %bitcast.40, bf16[2048,384]{1,0:T(8,128)(2,1)} %bitcast.5.source_ref, ...), custom_call_target="tpu_custom_call" | custom-call | flops 3221225472 | bytes 16777216 | tf_op jit(solution)/shard_map/pallas_call | solution.py:118
  35.3 7.5 %collective-permute-done.6 = bf16[3,128,384]{2,1,0:T(8,128)(2,1)S(1)} collective-permute-done((bf16[3,128,384]{2,1,0:T(8,128)(2,1)}, bf16[3,128,384]{2,1,0:T(8,128)(2,1)S(1)}, u32[]{:S(2)}, u32[]{:S(2)}) %collective-permute-start.6) | collective-permute-done | bytes 294944 | tf_op jit(solution)/shard_map/ppermute | solution.py:254
  42.9 0.1 broadcast_select_fusion.1
  43.0 3.2 %shard_map.87 = bf16[2048,384]{1,0:T(8,128)(2,1)S(1)} custom-call(bf16[640,2048]{1,0:T(8,128)(2,1)S(1)} %get-tuple-element.14.close_ref, bf16[384,1024]{1,0:T(8,128)(2,1)S(1)} %get-tuple-element.15.far_ref, f32[2048,384]{1,0:T(8,128)S(1)} %get-tuple-element.16.partial_ref, bf16[640,384]{1,0:T(8,128)(2,1)} %bitcast.8.low_close_ref, ...), custom_call_target="tpu_custom_call" | custom-call | flops 1006632960 | bytes 10485760 | tf_op jit(solution)/shard_map/pallas_call | solution.py:160
  46.2 0.0 copy-start.5
  46.2 33.1 %all_to_all.25 = bf16[16,128,384]{2,1,0:T(8,128)(2,1)S(1)} all-to-all(bf16[16,128,384]{2,1,0:T(8,128)(2,1)S(1)} %bitcast.28), channel_id=1, replica_groups=mesh['comp'=2,'lat'=16,'lon'=8] {'lon'}, dimensions={0} | all-to-all | bytes 3145728 | tf_op jit(solution)/shard_map/all_to_all | solution.py:216
  79.3 6.1 %shard_map.88 = (bf16[8,2,128,384]{3,2,1,0:T(8,128)(2,1)}, bf16[384,384]{1,0:T(8,128)(2,1)S(1)}) custom-call(bf16[1024,1024]{1,0:T(8,128)(2,1)S(1)} %copy-done.5, bf16[8,2,128,384]{3,2,1,0:T(8,128)(2,1)S(1)} %bitcast.30, bf16[8,2,128,384]{3,2,1,0:T(8,128)(2,1)S(1)} %bitcast.29, bf16[384,384]{1,0:T(8,128)(2,1)S(1)} %bitcast.37), custom_call_target="tpu_custom_call" | custom-call | flops 2818572288 | bytes 8388608 | tf_op jit(solution)/shard_map/pallas_call | solution.py:198
  85.3 10.2 %all_to_all.26 = bf16[8,48,384]{2,1,0:T(8,128)(2,1)S(1)} all-to-all(bf16[8,48,384]{2,1,0:T(8,128)(2,1)S(1)} %bitcast.36), channel_id=1, replica_groups=mesh['comp'=2,'lat'=16,'lon'=8] {'lon'}, dimensions={0} | all-to-all | bytes 589824 | tf_op jit(solution)/shard_map/all_to_all | solution.py:216
  95.5 3.6 %all-to-all-start.3 = ((bf16[16,128,384]{2,1,0:T(8,128)(2,1)}), bf16[16,128,384]{2,1,0:T(8,128)(2,1)S(1)}, u32[]{:S(2)}, u32[]{:S(2)}) async-start(bf16[16,128,384]{2,1,0:T(8,128)(2,1)} %bitcast.18), calls=%async_computation.3 | async-start | bytes 3145728 | tf_op jit(solution)/shard_map/all_to_all | solution.py:216
  99.1 0.1 collective-permute-start.7
  99.2 3.9 %collective-permute-done.7 = bf16[48,384]{1,0:T(8,128)(2,1)S(1)} collective-permute-done((bf16[48,384]{1,0:T(8,128)(2,1)S(1)}, bf16[48,384]{1,0:T(8,128)(2,1)S(1)}, u32[]{:S(2)}, u32[]{:S(2)}) %collective-permute-start.7) | collective-permute-done | bytes 36896 | tf_op jit(solution)/shard_map/ppermute | solution.py:225
  103.2 0.1 collective-permute-start.8
  103.3 5.2 %collective-permute-done.8 = bf16[48,384]{1,0:T(8,128)(2,1)S(1)} collective-permute-done((bf16[48,384]{1,0:T(8,128)(2,1)S(1)}, bf16[48,384]{1,0:T(8,128)(2,1)S(1)}, u32[]{:S(2)}, u32[]{:S(2)}) %collective-permute-start.8) | collective-permute-done | bytes 36896 | tf_op jit(solution)/shard_map/ppermute | solution.py:225
  108.5 3.7 %collective-permute-start.9 = (bf16[48,384]{1,0:T(8,128)(2,1)S(1)}, bf16[48,384]{1,0:T(8,128)(2,1)S(1)}, u32[]{:S(2)}, u32[]{:S(2)}) collective-permute-start(bf16[48,384]{1,0:T(8,128)(2,1)S(1)} %add_convert_fusion.2), channel_id=1, source_target_pairs={{0,32},{8,40},{16,48},{24,56},{32,0},{40,8},{48,16},{56,24},{64,96... | collective-permute-start | bytes 110600 | tf_op jit(solution)/shard_map/ppermute | solution.py:225
  112.2 3.4 %collective-permute-done.9 = bf16[48,384]{1,0:T(8,128)(2,1)S(1)} collective-permute-done((bf16[48,384]{1,0:T(8,128)(2,1)S(1)}, bf16[48,384]{1,0:T(8,128)(2,1)S(1)}, u32[]{:S(2)}, u32[]{:S(2)}) %collective-permute-start.9) | collective-permute-done | bytes 36896 | tf_op jit(solution)/shard_map/ppermute | solution.py:225
  115.6 3.1 %collective-permute-start.10 = (bf16[48,384]{1,0:T(8,128)(2,1)S(1)}, bf16[48,384]{1,0:T(8,128)(2,1)S(1)}, u32[]{:S(2)}, u32[]{:S(2)}) collective-permute-start(bf16[48,384]{1,0:T(8,128)(2,1)S(1)} %add_convert_fusion.1), channel_id=1, source_target_pairs={{0,96},{8,104},{16,112},{24,120},{32,64},{40,72},{48,80},{56,88},{... | collective-permute-start | bytes 110600 | tf_op jit(solution)/shard_map/ppermute | solution.py:225
  118.7 3.0 %collective-permute-done.10 = bf16[48,384]{1,0:T(8,128)(2,1)S(1)} collective-permute-done((bf16[48,384]{1,0:T(8,128)(2,1)S(1)}, bf16[48,384]{1,0:T(8,128)(2,1)S(1)}, u32[]{:S(2)}, u32[]{:S(2)}) %collective-permute-start.10) | collective-permute-done | bytes 36896 | tf_op jit(solution)/shard_map/ppermute | solution.py:225
  121.8 0.7 broadcast_in_dim.16
  122.5 9.5 %all-to-all-start.4 = ((bf16[8,48,384]{2,1,0:T(8,128)(2,1)}), bf16[8,48,384]{2,1,0:T(8,128)(2,1)S(1)}, u32[]{:S(2)}, u32[]{:S(2)}) async-start(bf16[8,48,384]{2,1,0:T(8,128)(2,1)} %broadcast_in_dim.16), calls=%async_computation.4 | async-start | bytes 589824 | tf_op jit(solution)/shard_map/all_to_all | solution.py:216
  132.0 1.3 select_bitcast_fusion
  133.3 6.2 %all-to-all-done.4 = bf16[8,48,384]{2,1,0:T(8,128)(2,1)S(1)} async-done(((bf16[8,48,384]{2,1,0:T(8,128)(2,1)}), bf16[8,48,384]{2,1,0:T(8,128)(2,1)S(1)}, u32[]{:S(2)}, u32[]{:S(2)}) %all-to-all-start.4) | async-done | bytes 294944 | tf_op jit(solution)/shard_map/all_to_all | solution.py:216
  139.5 0.9 bitcast_convert_fusion
  (25 shorter events, 0.2 us)
Async XLA Ops:
  0.6 5.9 %collective-permute-start = (bf16[16,128,384]{2,1,0:T(8,128)(2,1)}, bf16[16,128,384]{2,1,0:T(8,128)(2,1)}, u32[]{:S(2)}, u32[]{:S(2)}) collective-permute-start(bf16[16,128,384]{2,1,0:T(8,128)(2,1)} %bitcast.31), channel_id=1, source_target_pairs={{0,128},{128,0},{1,129},{129,1},{2,130},{130,2},{3,131},{131,3},{4... | collective-permute-start | bytes 4718600 | tf_op jit(solution)/shard_map/ppermute | solution.py:289
  0.7 5.8 %copy-start = (bf16[1,16,128,384]{3,2,1,0:T(8,128)(2,1)S(1)}, bf16[1,16,128,384]{3,2,1,0:T(8,128)(2,1)}, u32[]{:S(2)}) copy-start(bf16[1,16,128,384]{3,2,1,0:T(8,128)(2,1)} %param.7) | copy-start | bytes 4718596
  0.7 45.4 %all-to-all-start.1 = ((bf16[16,128,384]{2,1,0:T(8,128)(2,1)}), bf16[16,128,384]{2,1,0:T(8,128)(2,1)S(1)}, u32[]{:S(2)}, u32[]{:S(2)}) async-start(bf16[16,128,384]{2,1,0:T(8,128)(2,1)} %bitcast.41), calls=%async_computation.1 | async-start | bytes 3145728 | tf_op jit(solution)/shard_map/all_to_all | solution.py:216
  6.5 17.7 %copy-start.2 = (s32[1,4,16,128]{3,2,1,0:T(8,128)S(1)}, s32[1,4,16,128]{3,2,1,0:T(8,128)}, u32[]{:S(2)}) copy-start(s32[1,4,16,128]{3,2,1,0:T(8,128)} %param.8) | copy-start | bytes 98308
  6.5 17.7 %copy-start.3 = (f32[1,4,16,128]{3,2,1,0:T(8,128)S(1)}, f32[1,4,16,128]{3,2,1,0:T(8,128)}, u32[]{:S(2)}) copy-start(f32[1,4,16,128]{3,2,1,0:T(8,128)} %param.9) | copy-start | bytes 98308
  6.6 17.7 %copy-start.4 = (s32[1,16,128]{2,1,0:T(8,128)S(1)}, s32[1,16,128]{2,1,0:T(8,128)}, u32[]{:S(2)}) copy-start(s32[1,16,128]{2,1,0:T(8,128)} %param.10) | copy-start | bytes 24580
  7.5 14.7 %collective-permute-start.5 = (bf16[3,128,384]{2,1,0:T(8,128)(2,1)}, bf16[3,128,384]{2,1,0:T(8,128)(2,1)}, u32[]{:S(2)}, u32[]{:S(2)}) collective-permute-start(bf16[3,128,384]{2,1,0:T(8,128)(2,1)} %get-tuple-element.24), channel_id=1, source_target_pairs={{8,128},{16,136},{24,144},{40,160},{48,168},{56,176},{72,192},{80,... | collective-permute-start | bytes 884744 | tf_op jit(solution)/shard_map/ppermute | solution.py:272
  10.7 12.9 %collective-permute-start.2 = (bf16[3,128,384]{2,1,0:T(8,128)(2,1)}, bf16[3,128,384]{2,1,0:T(8,128)(2,1)S(1)}, u32[]{:S(2)}, u32[]{:S(2)}) collective-permute-start(bf16[3,128,384]{2,1,0:T(8,128)(2,1)} %get-tuple-element.25), channel_id=1, source_target_pairs={{0,136},{8,144},{16,152},{32,168},{40,176},{48,184},{64,200},{72,2... | collective-permute-start | bytes 884744 | tf_op jit(solution)/shard_map/ppermute | solution.py:271
  13.6 29.3 %collective-permute-start.4 = (bf16[5,128,384]{2,1,0:T(8,128)(2,1)}, bf16[5,128,384]{2,1,0:T(8,128)(2,1)}, u32[]{:S(2)}, u32[]{:S(2)}) collective-permute-start(bf16[5,128,384]{2,1,0:T(8,128)(2,1)} %get-tuple-element.26), channel_id=1, source_target_pairs={{8,128},{16,136},{24,144},{32,152},{40,160},{48,168},{56,176},{64,... | collective-permute-start | bytes 1474568 | tf_op jit(solution)/shard_map/ppermute | solution.py:254
  17.3 25.7 %collective-permute-start.1 = (bf16[5,128,384]{2,1,0:T(8,128)(2,1)}, bf16[5,128,384]{2,1,0:T(8,128)(2,1)}, u32[]{:S(2)}, u32[]{:S(2)}) collective-permute-start(bf16[5,128,384]{2,1,0:T(8,128)(2,1)} %get-tuple-element.27), channel_id=1, source_target_pairs={{0,136},{8,144},{16,152},{24,160},{32,168},{40,176},{48,184},{56,1... | collective-permute-start | bytes 1474568 | tf_op jit(solution)/shard_map/ppermute | solution.py:254
  22.2 20.6 %collective-permute-start.6 = (bf16[3,128,384]{2,1,0:T(8,128)(2,1)}, bf16[3,128,384]{2,1,0:T(8,128)(2,1)S(1)}, u32[]{:S(2)}, u32[]{:S(2)}) collective-permute-start(bf16[3,128,384]{2,1,0:T(8,128)(2,1)} %collective-permute-done.5), channel_id=1, source_target_pairs={{56,152},{88,184},{120,216},{184,24},{216,56},{248,88},{57,153},{8... | collective-permute-start | bytes 884744 | tf_op jit(solution)/shard_map/ppermute | solution.py:254
  23.5 19.4 %collective-permute-start.3 = (bf16[3,128,384]{2,1,0:T(8,128)(2,1)S(1)}, bf16[3,128,384]{2,1,0:T(8,128)(2,1)S(1)}, u32[]{:S(2)}, u32[]{:S(2)}) collective-permute-start(bf16[3,128,384]{2,1,0:T(8,128)(2,1)S(1)} %collective-permute-done.2), channel_id=1, source_target_pairs={{0,160},{32,192},{64,224},{128,32},{160,64},{192,96},{1,161},{33,1... | collective-permute-start | bytes 884744 | tf_op jit(solution)/shard_map/ppermute | solution.py:254
  46.2 33.1 %copy-start.1 = (bf16[1,384,384]{2,1,0:T(8,128)(2,1)S(1)}, bf16[1,384,384]{2,1,0:T(8,128)(2,1)}, u32[]{:S(2)}) copy-start(bf16[1,384,384]{2,1,0:T(8,128)(2,1)} %param.11) | copy-start | bytes 884740
  46.2 33.1 %copy-start.5 = (bf16[1024,1024]{1,0:T(8,128)(2,1)S(1)}, bf16[1024,1024]{1,0:T(8,128)(2,1)}, u32[]{:S(2)}) copy-start(bf16[1024,1024]{1,0:T(8,128)(2,1)} %constant.29.clone.filter_ref) | copy-start | bytes 6291460
  95.5 26.3 %all-to-all-start.3 = ((bf16[16,128,384]{2,1,0:T(8,128)(2,1)}), bf16[16,128,384]{2,1,0:T(8,128)(2,1)S(1)}, u32[]{:S(2)}, u32[]{:S(2)}) async-start(bf16[16,128,384]{2,1,0:T(8,128)(2,1)} %bitcast.18), calls=%async_computation.3 | async-start | bytes 3145728 | tf_op jit(solution)/shard_map/all_to_all | solution.py:216
  99.1 4.0 %collective-permute-start.7 = (bf16[48,384]{1,0:T(8,128)(2,1)S(1)}, bf16[48,384]{1,0:T(8,128)(2,1)S(1)}, u32[]{:S(2)}, u32[]{:S(2)}) collective-permute-start(bf16[48,384]{1,0:T(8,128)(2,1)S(1)} %reduce_sum.12), channel_id=1, source_target_pairs={{0,8},{8,0},{16,24},{24,16},{32,40},{40,32},{48,56},{56,48},{64,72... | collective-permute-start | bytes 110600 | tf_op jit(solution)/shard_map/ppermute | solution.py:225
  103.2 5.3 %collective-permute-start.8 = (bf16[48,384]{1,0:T(8,128)(2,1)S(1)}, bf16[48,384]{1,0:T(8,128)(2,1)S(1)}, u32[]{:S(2)}, u32[]{:S(2)}) collective-permute-start(bf16[48,384]{1,0:T(8,128)(2,1)S(1)} %add_convert_fusion.3), channel_id=1, source_target_pairs={{0,24},{8,16},{16,8},{24,0},{32,56},{40,48},{48,40},{56,32},{64,88... | collective-permute-start | bytes 110600 | tf_op jit(solution)/shard_map/ppermute | solution.py:225
  108.5 7.1 %collective-permute-start.9 = (bf16[48,384]{1,0:T(8,128)(2,1)S(1)}, bf16[48,384]{1,0:T(8,128)(2,1)S(1)}, u32[]{:S(2)}, u32[]{:S(2)}) collective-permute-start(bf16[48,384]{1,0:T(8,128)(2,1)S(1)} %add_convert_fusion.2), channel_id=1, source_target_pairs={{0,32},{8,40},{16,48},{24,56},{32,0},{40,8},{48,16},{56,24},{64,96... | collective-permute-start | bytes 110600 | tf_op jit(solution)/shard_map/ppermute | solution.py:225
  115.6 6.2 %collective-permute-start.10 = (bf16[48,384]{1,0:T(8,128)(2,1)S(1)}, bf16[48,384]{1,0:T(8,128)(2,1)S(1)}, u32[]{:S(2)}, u32[]{:S(2)}) collective-permute-start(bf16[48,384]{1,0:T(8,128)(2,1)S(1)} %add_convert_fusion.1), channel_id=1, source_target_pairs={{0,96},{8,104},{16,112},{24,120},{32,64},{40,72},{48,80},{56,88},{... | collective-permute-start | bytes 110600 | tf_op jit(solution)/shard_map/ppermute | solution.py:225
  122.5 16.9 %all-to-all-start.4 = ((bf16[8,48,384]{2,1,0:T(8,128)(2,1)}), bf16[8,48,384]{2,1,0:T(8,128)(2,1)S(1)}, u32[]{:S(2)}, u32[]{:S(2)}) async-start(bf16[8,48,384]{2,1,0:T(8,128)(2,1)} %broadcast_in_dim.16), calls=%async_computation.4 | async-start | bytes 589824 | tf_op jit(solution)/shard_map/all_to_all | solution.py:216
where the time goes:
time: 141 us; the launch traced here: 140 us
  blocking collectives  43.3 us (31%)
  starting transfers between devices  41.6 us (30%)
  waiting for transfers between devices  29.2 us (21%)
  Pallas kernels  20.3 us (14%)
  local copies, waits for them, and re-layouts  2.72 us (2%)
  other arithmetic  2.34 us (2%)
    all_to_all x2, blocking collectives, spread(): return lax.all_to_all(block, axis, split_axis=0, concat_axis=0, tiled=True)  43.3 us
    all_to_all x3, starting transfers between devices, spread(): return lax.all_to_all(block, axis, split_axis=0, concat_axis=0, tiled=True)  18.9 us
    ppermute x4, waiting for transfers between devices, fold(): other = lax.ppermute(piece, 'lat', pairs)  15.5 us
    pallas_call x1, Pallas kernels, near_part(): pl.pallas_call(near_kernel, out_shape=(jax.ShapeDtypeStruct((targets, cha...  11.1 us
    ppermute x4, starting transfers between devices, send(): lax.ppermute(block, ('comp', 'lat'), route(pairs, lax.axis_size('lat'), s...  10.5 us
    ppermute x4, waiting for transfers between devices, send(): lax.ppermute(block, ('comp', 'lat'), route(pairs, lax.axis_size('lat'), s...  7.54 us
    ppermute x4, starting transfers between devices, fold(): other = lax.ppermute(piece, 'lat', pairs)  7.04 us
    all_to_all x3, waiting for transfers between devices, spread(): return lax.all_to_all(block, axis, split_axis=0, concat_axis=0, tiled=True)  6.17 us
  transfers between devices with their start and end apart: 14, of which 6 were waited for; matrix products, arithmetic and copies ran while one was open for 2% of the time, Pallas kernels for 10%

commit v1 on v0

--- a/solution.py
+++ b/solution.py
@@ -226,6 +226,17 @@
     return (piece.astype(jnp.float32) + other.astype(jnp.float32)).astype(jnp.bfloat16)
 
 
+def gather_sum(piece, step):
+    parts = [piece.astype(jnp.float32)]
+    for shift in range(1, RING):
+        pairs = []
+        for place in range(lax.axis_size("lat")):
+            at = place // step % RING
+            pairs.append((place, place + ((at + shift) % RING - at) * step))
+        parts.append(lax.ppermute(piece, "lat", pairs).astype(jnp.float32))
+    return ((parts[0] + parts[2]) + (parts[1] + parts[3])).astype(jnp.bfloat16)
+
+
 def finish(updated, grad):
     rows, columns = grad.shape
     count = lax.axis_size("lon")
@@ -233,8 +244,8 @@
     updated, pieces = lax.optimization_barrier((updated, pieces))
     updated = spread(updated, "lon")
     piece = jnp.sum(pieces.astype(jnp.float32), axis=0).astype(jnp.bfloat16)
-    piece = fold(fold(piece, 1, 0), 1, 1)
-    piece = fold(fold(piece, RING, 0), RING, 1)
+    piece = gather_sum(piece, 1)
+    piece = gather_sum(piece, RING)
     updated, piece = lax.optimization_barrier((updated, piece))
     copies = jnp.broadcast_to(piece[None], (count, *piece.shape))
     total = spread(copies, "lon").reshape(rows, columns).astype(jnp.float32)

time: 141 us -> 138 us (0.979)
  waiting for transfers between devices: 29.2 us -> 21.6 us
  starting transfers between devices: 41.6 us -> 45.4 us
    ppermute x4 -> x6, waiting for transfers between devices: 15.5 us -> 6.87 us  [gather_sum(): parts.append(lax.ppermute(piece, 'lat', pairs).astype(jnp.float32))]
    ppermute x4 -> x6, starting transfers between devices: 7.04 us -> 13.2 us  [gather_sum(): parts.append(lax.ppermute(piece, 'lat', pairs).astype(jnp.float32))]
    all_to_all x3, starting transfers between devices: 18.9 us -> 16.5 us  [spread(): return lax.all_to_all(block, axis, split_axis=0, concat_axis=0, tiled=True)]
  transfers between devices with their start and end apart: 14 -> 16, of which waited for: 6 -> 6; matrix products, arithmetic and copies ran while one was open for 2% -> 3% of each run, Pallas kernels for 10% -> 10%
where the time goes in v1:
time: 138 us; the launch traced here: 136 us
  starting transfers between devices  45.4 us (33%)
  blocking collectives  43.2 us (31%)
  waiting for transfers between devices  21.6 us (16%)
  Pallas kernels  20.3 us (15%)
  local copies, waits for them, and re-layouts  2.73 us (2%)
  other arithmetic  2.33 us (2%)
    all_to_all x2, blocking collectives, spread(): return lax.all_to_all(block, axis, split_axis=0, concat_axis=0, tiled=True)  43.2 us
    all_to_all x3, starting transfers between devices, spread(): return lax.all_to_all(block, axis, split_axis=0, concat_axis=0, tiled=True)  16.5 us
    ppermute x6, starting transfers between devices, gather_sum(): parts.append(lax.ppermute(piece, 'lat', pairs).astype(jnp.float32))  13.2 us
    pallas_call x1, Pallas kernels, near_part(): pl.pallas_call(near_kernel, out_shape=(jax.ShapeDtypeStruct((targets, cha...  11.1 us
    ppermute x4, starting transfers between devices, send(): lax.ppermute(block, ('comp', 'lat'), route(pairs, lax.axis_size('lat'), s...  10.5 us
    ppermute x4, waiting for transfers between devices, send(): lax.ppermute(block, ('comp', 'lat'), route(pairs, lax.axis_size('lat'), s...  7.54 us
    all_to_all x3, waiting for transfers between devices, spread(): return lax.all_to_all(block, axis, split_axis=0, concat_axis=0, tiled=True)  7.2 us
    ppermute x6, waiting for transfers between devices, gather_sum(): parts.append(lax.ppermute(piece, 'lat', pairs).astype(jnp.float32))  6.87 us
  transfers between devices with their start and end apart: 16, of which 6 were waited for; matrix products, arithmetic and copies ran while one was open for 3% of the time, Pallas kernels for 10%

profile of v1, /device:TPU:24, one launch (start us, length us, event | category | flops | bytes accessed | tf_op | source)
XLA Modules:
  0.0 136.5 jit_solution(1231147000735798163)
XLA Ops:
  0.6 0.1 collective-permute-start
  0.7 5.8 %all-to-all-start.1 = ((bf16[16,128,384]{2,1,0:T(8,128)(2,1)}), bf16[16,128,384]{2,1,0:T(8,128)(2,1)S(1)}, u32[]{:S(2)}, u32[]{:S(2)}) async-start(bf16[16,128,384]{2,1,0:T(8,128)(2,1)} %bitcast.41), calls=%async_computation.1 | async-start | bytes 3145728 | tf_op jit(solution)/shard_map/all_to_all | solution.py:216
  6.6 0.9 fusion
  7.5 3.2 %collective-permute-start.5 = (bf16[3,128,384]{2,1,0:T(8,128)(2,1)}, bf16[3,128,384]{2,1,0:T(8,128)(2,1)}, u32[]{:S(2)}, u32[]{:S(2)}) collective-permute-start(bf16[3,128,384]{2,1,0:T(8,128)(2,1)} %get-tuple-element.24), channel_id=1, source_target_pairs={{8,128},{16,136},{24,144},{40,160},{48,168},{56,176},{72,192},{80,... | collective-permute-start | bytes 884744 | tf_op jit(solution)/shard_map/ppermute | solution.py:283
  10.7 1.9 %collective-permute-start.2 = (bf16[3,128,384]{2,1,0:T(8,128)(2,1)}, bf16[3,128,384]{2,1,0:T(8,128)(2,1)S(1)}, u32[]{:S(2)}, u32[]{:S(2)}) collective-permute-start(bf16[3,128,384]{2,1,0:T(8,128)(2,1)} %get-tuple-element.25), channel_id=1, source_target_pairs={{0,136},{8,144},{16,152},{32,168},{40,176},{48,184},{64,200},{72,2... | collective-permute-start | bytes 884744 | tf_op jit(solution)/shard_map/ppermute | solution.py:282
  12.6 1.1 slice_bitcast_fusion
  13.6 3.6 %collective-permute-start.4 = (bf16[5,128,384]{2,1,0:T(8,128)(2,1)}, bf16[5,128,384]{2,1,0:T(8,128)(2,1)}, u32[]{:S(2)}, u32[]{:S(2)}) collective-permute-start(bf16[5,128,384]{2,1,0:T(8,128)(2,1)} %get-tuple-element.26), channel_id=1, source_target_pairs={{8,128},{16,136},{24,144},{32,152},{40,160},{48,168},{56,176},{64,... | collective-permute-start | bytes 1474568 | tf_op jit(solution)/shard_map/ppermute | solution.py:265
  17.3 4.9 %collective-permute-start.1 = (bf16[5,128,384]{2,1,0:T(8,128)(2,1)}, bf16[5,128,384]{2,1,0:T(8,128)(2,1)}, u32[]{:S(2)}, u32[]{:S(2)}) collective-permute-start(bf16[5,128,384]{2,1,0:T(8,128)(2,1)} %get-tuple-element.27), channel_id=1, source_target_pairs={{0,136},{8,144},{16,152},{24,160},{32,168},{40,176},{48,184},{56,1... | collective-permute-start | bytes 1474568 | tf_op jit(solution)/shard_map/ppermute | solution.py:265
  22.2 1.3 collective-permute-start.6
  23.5 0.7 collective-permute-start.3
  24.3 11.1 %shard_map.86 = (f32[2048,384]{1,0:T(8,128)S(1)}, bf16[640,2048]{1,0:T(8,128)(2,1)S(1)}, bf16[384,1024]{1,0:T(8,128)(2,1)S(1)}) custom-call(s32[1]{0:T(128)} %bitcast.lat_ref, s32[4,16,128]{2,1,0:T(8,128)S(1)} %bitcast.38, f32[4,16,128]{2,1,0:T(8,128)S(1)} %bitcast.39, s32[16,128]{1,0:T(8,128)S(1)} %bitcast.40, bf16[2048,384]{1,0:T(8,128)(2,1)} %bitcast.5.source_ref, ...), custom_call_target="tpu_custom_call" | custom-call | flops 3221225472 | bytes 16777216 | tf_op jit(solution)/shard_map/pallas_call | solution.py:118
  35.3 7.5 %collective-permute-done.6 = bf16[3,128,384]{2,1,0:T(8,128)(2,1)S(1)} collective-permute-done((bf16[3,128,384]{2,1,0:T(8,128)(2,1)}, bf16[3,128,384]{2,1,0:T(8,128)(2,1)S(1)}, u32[]{:S(2)}, u32[]{:S(2)}) %collective-permute-start.6) | collective-permute-done | bytes 294944 | tf_op jit(solution)/shard_map/ppermute | solution.py:265
  43.0 3.2 %shard_map.87 = bf16[2048,384]{1,0:T(8,128)(2,1)S(1)} custom-call(bf16[640,2048]{1,0:T(8,128)(2,1)S(1)} %get-tuple-element.14.close_ref, bf16[384,1024]{1,0:T(8,128)(2,1)S(1)} %get-tuple-element.15.far_ref, f32[2048,384]{1,0:T(8,128)S(1)} %get-tuple-element.16.partial_ref, bf16[640,384]{1,0:T(8,128)(2,1)} %bitcast.8.low_close_ref, ...), custom_call_target="tpu_custom_call" | custom-call | flops 1006632960 | bytes 10485760 | tf_op jit(solution)/shard_map/pallas_call | solution.py:160
  46.2 33.1 %all_to_all.25 = bf16[16,128,384]{2,1,0:T(8,128)(2,1)S(1)} all-to-all(bf16[16,128,384]{2,1,0:T(8,128)(2,1)S(1)} %bitcast.28), channel_id=1, replica_groups=mesh['comp'=2,'lat'=16,'lon'=8] {'lon'}, dimensions={0} | all-to-all | bytes 3145728 | tf_op jit(solution)/shard_map/all_to_all | solution.py:216
  79.3 6.1 %shard_map.88 = (bf16[8,2,128,384]{3,2,1,0:T(8,128)(2,1)}, bf16[384,384]{1,0:T(8,128)(2,1)S(1)}) custom-call(bf16[1024,1024]{1,0:T(8,128)(2,1)S(1)} %copy-done.5, bf16[8,2,128,384]{3,2,1,0:T(8,128)(2,1)S(1)} %bitcast.30, bf16[8,2,128,384]{3,2,1,0:T(8,128)(2,1)S(1)} %bitcast.29, bf16[384,384]{1,0:T(8,128)(2,1)S(1)} %bitcast.37), custom_call_target="tpu_custom_call" | custom-call | flops 2818572288 | bytes 8388608 | tf_op jit(solution)/shard_map/pallas_call | solution.py:198
  85.3 10.2 %all_to_all.26 = bf16[8,48,384]{2,1,0:T(8,128)(2,1)S(1)} all-to-all(bf16[8,48,384]{2,1,0:T(8,128)(2,1)S(1)} %bitcast.36), channel_id=1, replica_groups=mesh['comp'=2,'lat'=16,'lon'=8] {'lon'}, dimensions={0} | all-to-all | bytes 589824 | tf_op jit(solution)/shard_map/all_to_all | solution.py:216
  95.5 3.6 %all-to-all-start.3 = ((bf16[16,128,384]{2,1,0:T(8,128)(2,1)}), bf16[16,128,384]{2,1,0:T(8,128)(2,1)S(1)}, u32[]{:S(2)}, u32[]{:S(2)}) async-start(bf16[16,128,384]{2,1,0:T(8,128)(2,1)} %bitcast.18), calls=%async_computation.3 | async-start | bytes 3145728 | tf_op jit(solution)/shard_map/all_to_all | solution.py:216
  99.1 0.1 collective-permute-start.7
  99.2 0.1 collective-permute-start.8
  99.3 2.0 %collective-permute-start.9 = (bf16[48,384]{1,0:T(8,128)(2,1)S(1)}, bf16[48,384]{1,0:T(8,128)(2,1)S(1)}, u32[]{:S(2)}, u32[]{:S(2)}) collective-permute-start(bf16[48,384]{1,0:T(8,128)(2,1)S(1)} %reduce_sum.12), channel_id=1, source_target_pairs={{0,24},{8,0},{16,8},{24,16},{32,56},{40,32},{48,40},{56,48},{64,88... | collective-permute-start | bytes 110600 | tf_op jit(solution)/shard_map/ppermute | solution.py:236
  101.3 3.3 %collective-permute-done.7 = bf16[48,384]{1,0:T(8,128)(2,1)S(1)} collective-permute-done((bf16[48,384]{1,0:T(8,128)(2,1)S(1)}, bf16[48,384]{1,0:T(8,128)(2,1)S(1)}, u32[]{:S(2)}, u32[]{:S(2)}) %collective-permute-start.7) | collective-permute-done | bytes 36896 | tf_op jit(solution)/shard_map/ppermute | solution.py:236
  104.7 0.6 collective-permute-done.9
  105.3 6.9 %collective-permute-start.10 = (bf16[48,384]{1,0:T(8,128)(2,1)S(1)}, bf16[48,384]{1,0:T(8,128)(2,1)S(1)}, u32[]{:S(2)}, u32[]{:S(2)}) collective-permute-start(bf16[48,384]{1,0:T(8,128)(2,1)S(1)} %add_convert_fusion.1), channel_id=1, source_target_pairs={{0,64},{8,72},{16,80},{24,88},{32,96},{40,104},{48,112},{56,120},{... | collective-permute-start | bytes 110600 | tf_op jit(solution)/shard_map/ppermute | solution.py:236
  112.2 1.1 collective-permute-start.11
  113.3 3.0 %collective-permute-start.12 = (bf16[48,384]{1,0:T(8,128)(2,1)S(1)}, bf16[48,384]{1,0:T(8,128)(2,1)S(1)}, u32[]{:S(2)}, u32[]{:S(2)}) collective-permute-start(bf16[48,384]{1,0:T(8,128)(2,1)S(1)} %add_convert_fusion.1), channel_id=1, source_target_pairs={{0,96},{8,104},{16,112},{24,120},{32,0},{40,8},{48,16},{56,24},{64... | collective-permute-start | bytes 110600 | tf_op jit(solution)/shard_map/ppermute | solution.py:236
  116.3 3.0 %collective-permute-done.10 = bf16[48,384]{1,0:T(8,128)(2,1)S(1)} collective-permute-done((bf16[48,384]{1,0:T(8,128)(2,1)S(1)}, bf16[48,384]{1,0:T(8,128)(2,1)S(1)}, u32[]{:S(2)}, u32[]{:S(2)}) %collective-permute-start.10) | collective-permute-done | bytes 36896 | tf_op jit(solution)/shard_map/ppermute | solution.py:236
  119.3 1.0 all-to-all-done.3
  120.3 0.7 broadcast_in_dim.16
  121.1 7.1 %all-to-all-start.4 = ((bf16[8,48,384]{2,1,0:T(8,128)(2,1)}), bf16[8,48,384]{2,1,0:T(8,128)(2,1)S(1)}, u32[]{:S(2)}, u32[]{:S(2)}) async-start(bf16[8,48,384]{2,1,0:T(8,128)(2,1)} %broadcast_in_dim.16), calls=%async_computation.4 | async-start | bytes 589824 | tf_op jit(solution)/shard_map/all_to_all | solution.py:216
  128.2 1.3 select_bitcast_fusion
  129.5 6.2 %all-to-all-done.4 = bf16[8,48,384]{2,1,0:T(8,128)(2,1)S(1)} async-done(((bf16[8,48,384]{2,1,0:T(8,128)(2,1)}), bf16[8,48,384]{2,1,0:T(8,128)(2,1)S(1)}, u32[]{:S(2)}, u32[]{:S(2)}) %all-to-all-start.4) | async-done | bytes 294944 | tf_op jit(solution)/shard_map/all_to_all | solution.py:216
  135.6 0.9 bitcast_convert_fusion
  (27 shorter events, 0.2 us)
Async XLA Ops:
  0.6 5.9 %collective-permute-start = (bf16[16,128,384]{2,1,0:T(8,128)(2,1)}, bf16[16,128,384]{2,1,0:T(8,128)(2,1)}, u32[]{:S(2)}, u32[]{:S(2)}) collective-permute-start(bf16[16,128,384]{2,1,0:T(8,128)(2,1)} %bitcast.31), channel_id=1, source_target_pairs={{0,128},{128,0},{1,129},{129,1},{2,130},{130,2},{3,131},{131,3},{4... | collective-permute-start | bytes 4718600 | tf_op jit(solution)/shard_map/ppermute | solution.py:300
  0.7 5.8 %copy-start = (bf16[1,16,128,384]{3,2,1,0:T(8,128)(2,1)S(1)}, bf16[1,16,128,384]{3,2,1,0:T(8,128)(2,1)}, u32[]{:S(2)}) copy-start(bf16[1,16,128,384]{3,2,1,0:T(8,128)(2,1)} %param.7) | copy-start | bytes 4718596
  0.7 45.4 %all-to-all-start.1 = ((bf16[16,128,384]{2,1,0:T(8,128)(2,1)}), bf16[16,128,384]{2,1,0:T(8,128)(2,1)S(1)}, u32[]{:S(2)}, u32[]{:S(2)}) async-start(bf16[16,128,384]{2,1,0:T(8,128)(2,1)} %bitcast.41), calls=%async_computation.1 | async-start | bytes 3145728 | tf_op jit(solution)/shard_map/all_to_all | solution.py:216
  6.5 17.7 %copy-start.2 = (s32[1,4,16,128]{3,2,1,0:T(8,128)S(1)}, s32[1,4,16,128]{3,2,1,0:T(8,128)}, u32[]{:S(2)}) copy-start(s32[1,4,16,128]{3,2,1,0:T(8,128)} %param.8) | copy-start | bytes 98308
  6.5 17.7 %copy-start.3 = (f32[1,4,16,128]{3,2,1,0:T(8,128)S(1)}, f32[1,4,16,128]{3,2,1,0:T(8,128)}, u32[]{:S(2)}) copy-start(f32[1,4,16,128]{3,2,1,0:T(8,128)} %param.9) | copy-start | bytes 98308
  6.6 17.7 %copy-start.4 = (s32[1,16,128]{2,1,0:T(8,128)S(1)}, s32[1,16,128]{2,1,0:T(8,128)}, u32[]{:S(2)}) copy-start(s32[1,16,128]{2,1,0:T(8,128)} %param.10) | copy-start | bytes 24580
  7.5 14.7 %collective-permute-start.5 = (bf16[3,128,384]{2,1,0:T(8,128)(2,1)}, bf16[3,128,384]{2,1,0:T(8,128)(2,1)}, u32[]{:S(2)}, u32[]{:S(2)}) collective-permute-start(bf16[3,128,384]{2,1,0:T(8,128)(2,1)} %get-tuple-element.24), channel_id=1, source_target_pairs={{8,128},{16,136},{24,144},{40,160},{48,168},{56,176},{72,192},{80,... | collective-permute-start | bytes 884744 | tf_op jit(solution)/shard_map/ppermute | solution.py:283
  10.7 12.9 %collective-permute-start.2 = (bf16[3,128,384]{2,1,0:T(8,128)(2,1)}, bf16[3,128,384]{2,1,0:T(8,128)(2,1)S(1)}, u32[]{:S(2)}, u32[]{:S(2)}) collective-permute-start(bf16[3,128,384]{2,1,0:T(8,128)(2,1)} %get-tuple-element.25), channel_id=1, source_target_pairs={{0,136},{8,144},{16,152},{32,168},{40,176},{48,184},{64,200},{72,2... | collective-permute-start | bytes 884744 | tf_op jit(solution)/shard_map/ppermute | solution.py:282
  13.6 29.3 %collective-permute-start.4 = (bf16[5,128,384]{2,1,0:T(8,128)(2,1)}, bf16[5,128,384]{2,1,0:T(8,128)(2,1)}, u32[]{:S(2)}, u32[]{:S(2)}) collective-permute-start(bf16[5,128,384]{2,1,0:T(8,128)(2,1)} %get-tuple-element.26), channel_id=1, source_target_pairs={{8,128},{16,136},{24,144},{32,152},{40,160},{48,168},{56,176},{64,... | collective-permute-start | bytes 1474568 | tf_op jit(solution)/shard_map/ppermute | solution.py:265
  17.3 25.7 %collective-permute-start.1 = (bf16[5,128,384]{2,1,0:T(8,128)(2,1)}, bf16[5,128,384]{2,1,0:T(8,128)(2,1)}, u32[]{:S(2)}, u32[]{:S(2)}) collective-permute-start(bf16[5,128,384]{2,1,0:T(8,128)(2,1)} %get-tuple-element.27), channel_id=1, source_target_pairs={{0,136},{8,144},{16,152},{24,160},{32,168},{40,176},{48,184},{56,1... | collective-permute-start | bytes 1474568 | tf_op jit(solution)/shard_map/ppermute | solution.py:265
  22.2 20.6 %collective-permute-start.6 = (bf16[3,128,384]{2,1,0:T(8,128)(2,1)}, bf16[3,128,384]{2,1,0:T(8,128)(2,1)S(1)}, u32[]{:S(2)}, u32[]{:S(2)}) collective-permute-start(bf16[3,128,384]{2,1,0:T(8,128)(2,1)} %collective-permute-done.5), channel_id=1, source_target_pairs={{56,152},{88,184},{120,216},{184,24},{216,56},{248,88},{57,153},{8... | collective-permute-start | bytes 884744 | tf_op jit(solution)/shard_map/ppermute | solution.py:265
  23.5 19.4 %collective-permute-start.3 = (bf16[3,128,384]{2,1,0:T(8,128)(2,1)S(1)}, bf16[3,128,384]{2,1,0:T(8,128)(2,1)S(1)}, u32[]{:S(2)}, u32[]{:S(2)}) collective-permute-start(bf16[3,128,384]{2,1,0:T(8,128)(2,1)S(1)} %collective-permute-done.2), channel_id=1, source_target_pairs={{0,160},{32,192},{64,224},{128,32},{160,64},{192,96},{1,161},{33,1... | collective-permute-start | bytes 884744 | tf_op jit(solution)/shard_map/ppermute | solution.py:265
  46.2 33.1 %copy-start.1 = (bf16[1,384,384]{2,1,0:T(8,128)(2,1)S(1)}, bf16[1,384,384]{2,1,0:T(8,128)(2,1)}, u32[]{:S(2)}) copy-start(bf16[1,384,384]{2,1,0:T(8,128)(2,1)} %param.11) | copy-start | bytes 884740
  46.2 33.1 %copy-start.5 = (bf16[1024,1024]{1,0:T(8,128)(2,1)S(1)}, bf16[1024,1024]{1,0:T(8,128)(2,1)}, u32[]{:S(2)}) copy-start(bf16[1024,1024]{1,0:T(8,128)(2,1)} %constant.29.clone.filter_ref) | copy-start | bytes 6291460
  95.5 24.8 %all-to-all-start.3 = ((bf16[16,128,384]{2,1,0:T(8,128)(2,1)}), bf16[16,128,384]{2,1,0:T(8,128)(2,1)S(1)}, u32[]{:S(2)}, u32[]{:S(2)}) async-start(bf16[16,128,384]{2,1,0:T(8,128)(2,1)} %bitcast.18), calls=%async_computation.3 | async-start | bytes 3145728 | tf_op jit(solution)/shard_map/all_to_all | solution.py:216
  99.1 5.5 %collective-permute-start.7 = (bf16[48,384]{1,0:T(8,128)(2,1)S(1)}, bf16[48,384]{1,0:T(8,128)(2,1)S(1)}, u32[]{:S(2)}, u32[]{:S(2)}) collective-permute-start(bf16[48,384]{1,0:T(8,128)(2,1)S(1)} %reduce_sum.12), channel_id=1, source_target_pairs={{0,16},{8,24},{16,0},{24,8},{32,48},{40,56},{48,32},{56,40},{64,80... | collective-permute-start | bytes 110600 | tf_op jit(solution)/shard_map/ppermute | solution.py:236
  99.2 5.5 %collective-permute-start.8 = (bf16[48,384]{1,0:T(8,128)(2,1)S(1)}, bf16[48,384]{1,0:T(8,128)(2,1)S(1)}, u32[]{:S(2)}, u32[]{:S(2)}) collective-permute-start(bf16[48,384]{1,0:T(8,128)(2,1)S(1)} %reduce_sum.12), channel_id=1, source_target_pairs={{0,8},{8,16},{16,24},{24,0},{32,40},{40,48},{48,56},{56,32},{64,72... | collective-permute-start | bytes 110600 | tf_op jit(solution)/shard_map/ppermute | solution.py:236
  99.3 5.9 %collective-permute-start.9 = (bf16[48,384]{1,0:T(8,128)(2,1)S(1)}, bf16[48,384]{1,0:T(8,128)(2,1)S(1)}, u32[]{:S(2)}, u32[]{:S(2)}) collective-permute-start(bf16[48,384]{1,0:T(8,128)(2,1)S(1)} %reduce_sum.12), channel_id=1, source_target_pairs={{0,24},{8,0},{16,8},{24,16},{32,56},{40,32},{48,40},{56,48},{64,88... | collective-permute-start | bytes 110600 | tf_op jit(solution)/shard_map/ppermute | solution.py:236
  105.3 14.0 %collective-permute-start.10 = (bf16[48,384]{1,0:T(8,128)(2,1)S(1)}, bf16[48,384]{1,0:T(8,128)(2,1)S(1)}, u32[]{:S(2)}, u32[]{:S(2)}) collective-permute-start(bf16[48,384]{1,0:T(8,128)(2,1)S(1)} %add_convert_fusion.1), channel_id=1, source_target_pairs={{0,64},{8,72},{16,80},{24,88},{32,96},{40,104},{48,112},{56,120},{... | collective-permute-start | bytes 110600 | tf_op jit(solution)/shard_map/ppermute | solution.py:236
  112.2 7.1 %collective-permute-start.11 = (bf16[48,384]{1,0:T(8,128)(2,1)S(1)}, bf16[48,384]{1,0:T(8,128)(2,1)S(1)}, u32[]{:S(2)}, u32[]{:S(2)}) collective-permute-start(bf16[48,384]{1,0:T(8,128)(2,1)S(1)} %add_convert_fusion.1), channel_id=1, source_target_pairs={{0,32},{8,40},{16,48},{24,56},{32,64},{40,72},{48,80},{56,88},{64,... | collective-permute-start | bytes 110600 | tf_op jit(solution)/shard_map/ppermute | solution.py:236
  113.3 6.0 %collective-permute-start.12 = (bf16[48,384]{1,0:T(8,128)(2,1)S(1)}, bf16[48,384]{1,0:T(8,128)(2,1)S(1)}, u32[]{:S(2)}, u32[]{:S(2)}) collective-permute-start(bf16[48,384]{1,0:T(8,128)(2,1)S(1)} %add_convert_fusion.1), channel_id=1, source_target_pairs={{0,96},{8,104},{16,112},{24,120},{32,0},{40,8},{48,16},{56,24},{64... | collective-permute-start | bytes 110600 | tf_op jit(solution)/shard_map/ppermute | solution.py:236
  121.1 14.6 %all-to-all-start.4 = ((bf16[8,48,384]{2,1,0:T(8,128)(2,1)}), bf16[8,48,384]{2,1,0:T(8,128)(2,1)S(1)}, u32[]{:S(2)}, u32[]{:S(2)}) async-start(bf16[8,48,384]{2,1,0:T(8,128)(2,1)} %broadcast_in_dim.16), calls=%async_computation.4 | async-start | bytes 589824 | tf_op jit(solution)/shard_map/all_to_all | solution.py:216

commit v2 on v1

--- a/solution.py
+++ b/solution.py
@@ -246,8 +246,8 @@
     piece = jnp.sum(pieces.astype(jnp.float32), axis=0).astype(jnp.bfloat16)
     piece = gather_sum(piece, 1)
     piece = gather_sum(piece, RING)
-    updated, piece = lax.optimization_barrier((updated, piece))
     copies = jnp.broadcast_to(piece[None], (count, *piece.shape))
+    updated, copies = lax.optimization_barrier((updated, copies))
     total = spread(copies, "lon").reshape(rows, columns).astype(jnp.float32)
     updated = jnp.where(lax.axis_index("lat") < lax.axis_size("lat"), updated, 0)
     return updated, total
@@ -271,7 +271,9 @@
     down = [(high, low) for low, high in up]
     low_close = send(own[lat_dev - CLOSE :], up, 1)
     high_close = send(own[:CLOSE], down, 1)
-    own, ready = lax.optimization_barrier((own, ready))
+    rows_up, rows_down, ready = lax.optimization_barrier(
+        (own[lat_dev - REACH : lat_dev - CLOSE], own[CLOSE:REACH], ready)
+    )
     inner = [pair for pair in up if pair[1] % RING]
     rings = range(0, lat_count - RING, RING)
     first_up = [(ring + RING - 1, ring) for ring in rings]
@@ -279,8 +281,8 @@
     turn = lambda pairs: [(high, low) for low, high in pairs]
     mixed = lambda pairs, relay: route(pairs, lat_count, 1) + route(relay, lat_count, 0)
     axes = ("comp", "lat")
-    far_up = lax.ppermute(own[lat_dev - REACH : lat_dev - CLOSE], axes, mixed(inner, first_up))
-    far_down = lax.ppermute(own[CLOSE:REACH], axes, mixed(turn(inner), first_down))
+    far_up = lax.ppermute(rows_up, axes, mixed(inner, first_up))
+    far_down = lax.ppermute(rows_down, axes, mixed(turn(inner), first_down))
     over_up = send(far_up, [(ring, ring + RING) for ring in rings], 1)
     over_down = send(far_down, [(ring + 2 * RING - 1, ring + RING - 1) for ring in rings], 1)
     place = lax.axis_index("lat") % RING

time: 138 us -> 138 us (level)
  waiting for transfers between devices: 21.6 us -> 28.5 us
  blocking collectives: 43.2 us -> 37.3 us
  starting transfers between devices: 45.4 us -> 44 us
    all_to_all x2, blocking collectives: 43.2 us -> 37.3 us  [spread(): return lax.all_to_all(block, axis, split_axis=0, concat_axis=0, tiled=True)]
    ppermute x4, waiting for transfers between devices: 7.54 us -> 12.2 us  [send(): lax.ppermute(block, ('comp', 'lat'), route(pairs, lax.axis_size('lat'), s...]
    ppermute x6, waiting for transfers between devices: 6.87 us -> 10.1 us  [gather_sum(): parts.append(lax.ppermute(piece, 'lat', pairs).astype(jnp.float32))]
    ppermute x6, starting transfers between devices: 13.2 us -> 11.7 us  [gather_sum(): parts.append(lax.ppermute(piece, 'lat', pairs).astype(jnp.float32))]
where the time goes in v2:
time: 138 us; the launch traced here: 137 us
  starting transfers between devices  44 us (32%)
  blocking collectives  37.3 us (27%)
  waiting for transfers between devices  28.5 us (21%)
  Pallas kernels  20.3 us (15%)
  other arithmetic  3.3 us (2%)
  local copies, waits for them, and re-layouts  2.73 us (2%)
    all_to_all x2, blocking collectives, spread(): return lax.all_to_all(block, axis, split_axis=0, concat_axis=0, tiled=True)  37.3 us
    all_to_all x3, starting transfers between devices, spread(): return lax.all_to_all(block, axis, split_axis=0, concat_axis=0, tiled=True)  17.1 us
    ppermute x4, waiting for transfers between devices, send(): lax.ppermute(block, ('comp', 'lat'), route(pairs, lax.axis_size('lat'), s...  12.2 us
    ppermute x6, starting transfers between devices, gather_sum(): parts.append(lax.ppermute(piece, 'lat', pairs).astype(jnp.float32))  11.7 us
    pallas_call x1, Pallas kernels, near_part(): pl.pallas_call(near_kernel, out_shape=(jax.ShapeDtypeStruct((targets, cha...  11.1 us
    ppermute x6, waiting for transfers between devices, gather_sum(): parts.append(lax.ppermute(piece, 'lat', pairs).astype(jnp.float32))  10.1 us
    ppermute x4, starting transfers between devices, send(): lax.ppermute(block, ('comp', 'lat'), route(pairs, lax.axis_size('lat'), s...  9.51 us
    all_to_all x3, waiting for transfers between devices, spread(): return lax.all_to_all(block, axis, split_axis=0, concat_axis=0, tiled=True)  6.19 us
  transfers between devices with their start and end apart: 16, of which 6 were waited for; matrix products, arithmetic and copies ran while one was open for 3% of the time, Pallas kernels for 10%

profile of v2, /device:TPU:24, one launch (start us, length us, event | category | flops | bytes accessed | tf_op | source)
XLA Modules:
  0.0 137.0 jit_solution(8830518401563747629)
XLA Ops:
  0.6 0.1 collective-permute-start
  0.7 5.8 %all-to-all-start.1 = ((bf16[16,128,384]{2,1,0:T(8,128)(2,1)}), bf16[16,128,384]{2,1,0:T(8,128)(2,1)S(1)}, u32[]{:S(2)}, u32[]{:S(2)}) async-start(bf16[16,128,384]{2,1,0:T(8,128)(2,1)} %bitcast.44), calls=%async_computation.1 | async-start | bytes 3145728 | tf_op jit(solution)/shard_map/all_to_all | solution.py:216
  6.6 0.9 slice_bitcast_fusion.2
  7.5 2.1 %collective-permute-start.2 = (bf16[3,128,384]{2,1,0:T(8,128)(2,1)}, bf16[3,128,384]{2,1,0:T(8,128)(2,1)}, u32[]{:S(2)}, u32[]{:S(2)}) collective-permute-start(bf16[3,128,384]{2,1,0:T(8,128)(2,1)} %get-tuple-element.18), channel_id=1, source_target_pairs={{0,136},{8,144},{16,152},{32,168},{40,176},{48,184},{64,200},{72,2... | collective-permute-start | bytes 884744 | tf_op jit(solution)/shard_map/ppermute | solution.py:284
  9.6 3.4 %collective-permute-start.5 = (bf16[3,128,384]{2,1,0:T(8,128)(2,1)}, bf16[3,128,384]{2,1,0:T(8,128)(2,1)S(1)}, u32[]{:S(2)}, u32[]{:S(2)}) collective-permute-start(bf16[3,128,384]{2,1,0:T(8,128)(2,1)} %get-tuple-element.19), channel_id=1, source_target_pairs={{8,128},{16,136},{24,144},{40,160},{48,168},{56,176},{72,192},{80,... | collective-permute-start | bytes 884744 | tf_op jit(solution)/shard_map/ppermute | solution.py:285
  13.1 1.1 slice_bitcast_fusion
  14.1 5.6 %collective-permute-start.1 = (bf16[5,128,384]{2,1,0:T(8,128)(2,1)}, bf16[5,128,384]{2,1,0:T(8,128)(2,1)}, u32[]{:S(2)}, u32[]{:S(2)}) collective-permute-start(bf16[5,128,384]{2,1,0:T(8,128)(2,1)} %get-tuple-element.27), channel_id=1, source_target_pairs={{0,136},{8,144},{16,152},{24,160},{32,168},{40,176},{48,184},{56,1... | collective-permute-start | bytes 1474568 | tf_op jit(solution)/shard_map/ppermute | solution.py:265
  19.7 1.9 %collective-permute-start.4 = (bf16[5,128,384]{2,1,0:T(8,128)(2,1)}, bf16[5,128,384]{2,1,0:T(8,128)(2,1)}, u32[]{:S(2)}, u32[]{:S(2)}) collective-permute-start(bf16[5,128,384]{2,1,0:T(8,128)(2,1)} %get-tuple-element.26), channel_id=1, source_target_pairs={{8,128},{16,136},{24,144},{32,152},{40,160},{48,168},{56,176},{64,... | collective-permute-start | bytes 1474568 | tf_op jit(solution)/shard_map/ppermute | solution.py:265
  21.7 0.7 collective-permute-start.3
  22.4 1.3 collective-permute-start.6
  23.7 11.1 %shard_map.86 = (f32[2048,384]{1,0:T(8,128)S(1)}, bf16[640,2048]{1,0:T(8,128)(2,1)S(1)}, bf16[384,1024]{1,0:T(8,128)(2,1)S(1)}) custom-call(s32[1]{0:T(128)} %bitcast.lat_ref, s32[4,16,128]{2,1,0:T(8,128)S(1)} %bitcast.41, f32[4,16,128]{2,1,0:T(8,128)S(1)} %bitcast.42, s32[16,128]{1,0:T(8,128)S(1)} %bitcast.43, bf16[2048,384]{1,0:T(8,128)(2,1)} %bitcast.7.source_ref, ...), custom_call_target="tpu_custom_call" | custom-call | flops 3221225472 | bytes 16777216 | tf_op jit(solution)/shard_map/pallas_call | solution.py:118
  34.8 1.0 broadcast_select_fusion.1
  35.8 6.3 %collective-permute-done.6 = bf16[3,128,384]{2,1,0:T(8,128)(2,1)S(1)} collective-permute-done((bf16[3,128,384]{2,1,0:T(8,128)(2,1)S(1)}, bf16[3,128,384]{2,1,0:T(8,128)(2,1)S(1)}, u32[]{:S(2)}, u32[]{:S(2)}) %collective-permute-start.6) | collective-permute-done | bytes 294944 | tf_op jit(solution)/shard_map/ppermute | solution.py:265
  42.1 5.9 %collective-permute-done.4 = bf16[5,128,384]{2,1,0:T(8,128)(2,1)} collective-permute-done((bf16[5,128,384]{2,1,0:T(8,128)(2,1)}, bf16[5,128,384]{2,1,0:T(8,128)(2,1)}, u32[]{:S(2)}, u32[]{:S(2)}) %collective-permute-start.4) | collective-permute-done | bytes 491552 | tf_op jit(solution)/shard_map/ppermute | solution.py:265
  48.0 3.2 %shard_map.87 = bf16[2048,384]{1,0:T(8,128)(2,1)S(1)} custom-call(bf16[640,2048]{1,0:T(8,128)(2,1)S(1)} %get-tuple-element.15.close_ref, bf16[384,1024]{1,0:T(8,128)(2,1)S(1)} %get-tuple-element.16.far_ref, f32[2048,384]{1,0:T(8,128)S(1)} %get-tuple-element.17.partial_ref, bf16[640,384]{1,0:T(8,128)(2,1)} %bitcast.10.low_close_ref, ...), custom_call_target="tpu_custom_call" | custom-call | flops 1006632960 | bytes 10485760 | tf_op jit(solution)/shard_map/pallas_call | solution.py:160
  51.2 26.7 %all_to_all.25 = bf16[16,128,384]{2,1,0:T(8,128)(2,1)S(1)} all-to-all(bf16[16,128,384]{2,1,0:T(8,128)(2,1)S(1)} %bitcast.32), channel_id=1, replica_groups=mesh['comp'=2,'lat'=16,'lon'=8] {'lon'}, dimensions={0} | all-to-all | bytes 3145728 | tf_op jit(solution)/shard_map/all_to_all | solution.py:216
  78.0 6.1 %shard_map.88 = (bf16[8,2,128,384]{3,2,1,0:T(8,128)(2,1)}, bf16[384,384]{1,0:T(8,128)(2,1)S(1)}) custom-call(bf16[1024,1024]{1,0:T(8,128)(2,1)S(1)} %copy-done.5, bf16[8,2,128,384]{3,2,1,0:T(8,128)(2,1)S(1)} %bitcast.34, bf16[8,2,128,384]{3,2,1,0:T(8,128)(2,1)S(1)} %bitcast.33, bf16[384,384]{1,0:T(8,128)(2,1)S(1)} %bitcast.40), custom_call_target="tpu_custom_call" | custom-call | flops 2818572288 | bytes 8388608 | tf_op jit(solution)/shard_map/pallas_call | solution.py:198
  84.0 10.6 %all_to_all.26 = bf16[8,48,384]{2,1,0:T(8,128)(2,1)S(1)} all-to-all(bf16[8,48,384]{2,1,0:T(8,128)(2,1)S(1)} %bitcast.39), channel_id=1, replica_groups=mesh['comp'=2,'lat'=16,'lon'=8] {'lon'}, dimensions={0} | all-to-all | bytes 589824 | tf_op jit(solution)/shard_map/all_to_all | solution.py:216
  94.6 3.6 %all-to-all-start.3 = ((bf16[16,128,384]{2,1,0:T(8,128)(2,1)}), bf16[16,128,384]{2,1,0:T(8,128)(2,1)S(1)}, u32[]{:S(2)}, u32[]{:S(2)}) async-start(bf16[16,128,384]{2,1,0:T(8,128)(2,1)} %bitcast.20), calls=%async_computation.3 | async-start | bytes 3145728 | tf_op jit(solution)/shard_map/all_to_all | solution.py:216
  98.3 0.1 collective-permute-start.7
  98.5 2.0 %collective-permute-start.9 = (bf16[48,384]{1,0:T(8,128)(2,1)S(1)}, bf16[48,384]{1,0:T(8,128)(2,1)S(1)}, u32[]{:S(2)}, u32[]{:S(2)}) collective-permute-start(bf16[48,384]{1,0:T(8,128)(2,1)S(1)} %reduce_sum.12), channel_id=1, source_target_pairs={{0,24},{8,0},{16,8},{24,16},{32,56},{40,32},{48,40},{56,48},{64,88... | collective-permute-start | bytes 110600 | tf_op jit(solution)/shard_map/ppermute | solution.py:236
  100.5 3.3 %collective-permute-done.7 = bf16[48,384]{1,0:T(8,128)(2,1)S(1)} collective-permute-done((bf16[48,384]{1,0:T(8,128)(2,1)S(1)}, bf16[48,384]{1,0:T(8,128)(2,1)S(1)}, u32[]{:S(2)}, u32[]{:S(2)}) %collective-permute-start.7) | collective-permute-done | bytes 36896 | tf_op jit(solution)/shard_map/ppermute | solution.py:236
  103.8 0.6 collective-permute-done.9
  104.4 5.4 %collective-permute-start.10 = (bf16[48,384]{1,0:T(8,128)(2,1)S(1)}, bf16[48,384]{1,0:T(8,128)(2,1)S(1)}, u32[]{:S(2)}, u32[]{:S(2)}) collective-permute-start(bf16[48,384]{1,0:T(8,128)(2,1)S(1)} %add_convert_fusion.1), channel_id=1, source_target_pairs={{0,64},{8,72},{16,80},{24,88},{32,96},{40,104},{48,112},{56,120},{... | collective-permute-start | bytes 110600 | tf_op jit(solution)/shard_map/ppermute | solution.py:236
  109.8 2.3 %collective-permute-start.11 = (bf16[48,384]{1,0:T(8,128)(2,1)S(1)}, bf16[48,384]{1,0:T(8,128)(2,1)S(1)}, u32[]{:S(2)}, u32[]{:S(2)}) collective-permute-start(bf16[48,384]{1,0:T(8,128)(2,1)S(1)} %add_convert_fusion.1), channel_id=1, source_target_pairs={{0,32},{8,40},{16,48},{24,56},{32,64},{40,72},{48,80},{56,88},{64,... | collective-permute-start | bytes 110600 | tf_op jit(solution)/shard_map/ppermute | solution.py:236
  112.1 1.8 %collective-permute-start.12 = (bf16[48,384]{1,0:T(8,128)(2,1)S(1)}, bf16[48,384]{1,0:T(8,128)(2,1)S(1)}, u32[]{:S(2)}, u32[]{:S(2)}) collective-permute-start(bf16[48,384]{1,0:T(8,128)(2,1)S(1)} %add_convert_fusion.1), channel_id=1, source_target_pairs={{0,96},{8,104},{16,112},{24,120},{32,0},{40,8},{48,16},{56,24},{64... | collective-permute-start | bytes 110600 | tf_op jit(solution)/shard_map/ppermute | solution.py:236
  113.9 6.2 %collective-permute-done.10 = bf16[48,384]{1,0:T(8,128)(2,1)S(1)} collective-permute-done((bf16[48,384]{1,0:T(8,128)(2,1)S(1)}, bf16[48,384]{1,0:T(8,128)(2,1)S(1)}, u32[]{:S(2)}, u32[]{:S(2)}) %collective-permute-start.10) | collective-permute-done | bytes 36896 | tf_op jit(solution)/shard_map/ppermute | solution.py:236
  120.2 0.7 broadcast_in_dim.14
  120.9 7.7 %all-to-all-start.4 = ((bf16[8,48,384]{2,1,0:T(8,128)(2,1)}), bf16[8,48,384]{2,1,0:T(8,128)(2,1)S(1)}, u32[]{:S(2)}, u32[]{:S(2)}) async-start(bf16[8,48,384]{2,1,0:T(8,128)(2,1)} %broadcast_in_dim.14), calls=%async_computation.4 | async-start | bytes 589824 | tf_op jit(solution)/shard_map/all_to_all | solution.py:216
  128.7 1.3 select_bitcast_fusion
  130.0 6.2 %all-to-all-done.4 = bf16[8,48,384]{2,1,0:T(8,128)(2,1)S(1)} async-done(((bf16[8,48,384]{2,1,0:T(8,128)(2,1)}), bf16[8,48,384]{2,1,0:T(8,128)(2,1)S(1)}, u32[]{:S(2)}, u32[]{:S(2)}) %all-to-all-start.4) | async-done | bytes 294944 | tf_op jit(solution)/shard_map/all_to_all | solution.py:216
  136.1 0.9 bitcast_convert_fusion
  (27 shorter events, 0.3 us)
Async XLA Ops:
  0.6 6.9 %collective-permute-start = (bf16[16,128,384]{2,1,0:T(8,128)(2,1)}, bf16[16,128,384]{2,1,0:T(8,128)(2,1)}, u32[]{:S(2)}, u32[]{:S(2)}) collective-permute-start(bf16[16,128,384]{2,1,0:T(8,128)(2,1)} %bitcast.35), channel_id=1, source_target_pairs={{0,128},{128,0},{1,129},{129,1},{2,130},{130,2},{3,131},{131,3},{4... | collective-permute-start | bytes 4718600 | tf_op jit(solution)/shard_map/ppermute | solution.py:302
  0.7 5.8 %copy-start = (bf16[1,16,128,384]{3,2,1,0:T(8,128)(2,1)S(1)}, bf16[1,16,128,384]{3,2,1,0:T(8,128)(2,1)}, u32[]{:S(2)}) copy-start(bf16[1,16,128,384]{3,2,1,0:T(8,128)(2,1)} %param.7) | copy-start | bytes 4718596
  0.7 50.5 %all-to-all-start.1 = ((bf16[16,128,384]{2,1,0:T(8,128)(2,1)}), bf16[16,128,384]{2,1,0:T(8,128)(2,1)S(1)}, u32[]{:S(2)}, u32[]{:S(2)}) async-start(bf16[16,128,384]{2,1,0:T(8,128)(2,1)} %bitcast.44), calls=%async_computation.1 | async-start | bytes 3145728 | tf_op jit(solution)/shard_map/all_to_all | solution.py:216
  6.5 17.2 %copy-start.2 = (s32[1,4,16,128]{3,2,1,0:T(8,128)S(1)}, s32[1,4,16,128]{3,2,1,0:T(8,128)}, u32[]{:S(2)}) copy-start(s32[1,4,16,128]{3,2,1,0:T(8,128)} %param.8) | copy-start | bytes 98308
  6.6 17.2 %copy-start.3 = (f32[1,4,16,128]{3,2,1,0:T(8,128)S(1)}, f32[1,4,16,128]{3,2,1,0:T(8,128)}, u32[]{:S(2)}) copy-start(f32[1,4,16,128]{3,2,1,0:T(8,128)} %param.9) | copy-start | bytes 98308
  6.6 17.2 %copy-start.4 = (s32[1,16,128]{2,1,0:T(8,128)S(1)}, s32[1,16,128]{2,1,0:T(8,128)}, u32[]{:S(2)}) copy-start(s32[1,16,128]{2,1,0:T(8,128)} %param.10) | copy-start | bytes 24580
  7.5 14.2 %collective-permute-start.2 = (bf16[3,128,384]{2,1,0:T(8,128)(2,1)}, bf16[3,128,384]{2,1,0:T(8,128)(2,1)}, u32[]{:S(2)}, u32[]{:S(2)}) collective-permute-start(bf16[3,128,384]{2,1,0:T(8,128)(2,1)} %get-tuple-element.18), channel_id=1, source_target_pairs={{0,136},{8,144},{16,152},{32,168},{40,176},{48,184},{64,200},{72,2... | collective-permute-start | bytes 884744 | tf_op jit(solution)/shard_map/ppermute | solution.py:284
  9.6 12.8 %collective-permute-start.5 = (bf16[3,128,384]{2,1,0:T(8,128)(2,1)}, bf16[3,128,384]{2,1,0:T(8,128)(2,1)S(1)}, u32[]{:S(2)}, u32[]{:S(2)}) collective-permute-start(bf16[3,128,384]{2,1,0:T(8,128)(2,1)} %get-tuple-element.19), channel_id=1, source_target_pairs={{8,128},{16,136},{24,144},{40,160},{48,168},{56,176},{72,192},{80,... | collective-permute-start | bytes 884744 | tf_op jit(solution)/shard_map/ppermute | solution.py:285
  14.1 28.0 %collective-permute-start.1 = (bf16[5,128,384]{2,1,0:T(8,128)(2,1)}, bf16[5,128,384]{2,1,0:T(8,128)(2,1)}, u32[]{:S(2)}, u32[]{:S(2)}) collective-permute-start(bf16[5,128,384]{2,1,0:T(8,128)(2,1)} %get-tuple-element.27), channel_id=1, source_target_pairs={{0,136},{8,144},{16,152},{24,160},{32,168},{40,176},{48,184},{56,1... | collective-permute-start | bytes 1474568 | tf_op jit(solution)/shard_map/ppermute | solution.py:265
  19.7 28.3 %collective-permute-start.4 = (bf16[5,128,384]{2,1,0:T(8,128)(2,1)}, bf16[5,128,384]{2,1,0:T(8,128)(2,1)}, u32[]{:S(2)}, u32[]{:S(2)}) collective-permute-start(bf16[5,128,384]{2,1,0:T(8,128)(2,1)} %get-tuple-element.26), channel_id=1, source_target_pairs={{8,128},{16,136},{24,144},{32,152},{40,160},{48,168},{56,176},{64,... | collective-permute-start | bytes 1474568 | tf_op jit(solution)/shard_map/ppermute | solution.py:265
  21.7 13.1 %collective-permute-start.3 = (bf16[3,128,384]{2,1,0:T(8,128)(2,1)}, bf16[3,128,384]{2,1,0:T(8,128)(2,1)S(1)}, u32[]{:S(2)}, u32[]{:S(2)}) collective-permute-start(bf16[3,128,384]{2,1,0:T(8,128)(2,1)} %collective-permute-done.2), channel_id=1, source_target_pairs={{0,160},{32,192},{64,224},{128,32},{160,64},{192,96},{1,161},{33,1... | collective-permute-start | bytes 884744 | tf_op jit(solution)/shard_map/ppermute | solution.py:265
  22.4 19.7 %collective-permute-start.6 = (bf16[3,128,384]{2,1,0:T(8,128)(2,1)S(1)}, bf16[3,128,384]{2,1,0:T(8,128)(2,1)S(1)}, u32[]{:S(2)}, u32[]{:S(2)}) collective-permute-start(bf16[3,128,384]{2,1,0:T(8,128)(2,1)S(1)} %collective-permute-done.5), channel_id=1, source_target_pairs={{56,152},{88,184},{120,216},{184,24},{216,56},{248,88},{57,153},{8... | collective-permute-start | bytes 884744 | tf_op jit(solution)/shard_map/ppermute | solution.py:265
  51.2 26.8 %copy-start.1 = (bf16[1,384,384]{2,1,0:T(8,128)(2,1)S(1)}, bf16[1,384,384]{2,1,0:T(8,128)(2,1)}, u32[]{:S(2)}) copy-start(bf16[1,384,384]{2,1,0:T(8,128)(2,1)} %param.11) | copy-start | bytes 884740
  51.2 26.7 %copy-start.5 = (bf16[1024,1024]{1,0:T(8,128)(2,1)S(1)}, bf16[1024,1024]{1,0:T(8,128)(2,1)}, u32[]{:S(2)}) copy-start(bf16[1024,1024]{1,0:T(8,128)(2,1)} %constant.29.clone.filter_ref) | copy-start | bytes 6291460
  94.6 25.6 %all-to-all-start.3 = ((bf16[16,128,384]{2,1,0:T(8,128)(2,1)}), bf16[16,128,384]{2,1,0:T(8,128)(2,1)S(1)}, u32[]{:S(2)}, u32[]{:S(2)}) async-start(bf16[16,128,384]{2,1,0:T(8,128)(2,1)} %bitcast.20), calls=%async_computation.3 | async-start | bytes 3145728 | tf_op jit(solution)/shard_map/all_to_all | solution.py:216
  98.3 5.5 %collective-permute-start.7 = (bf16[48,384]{1,0:T(8,128)(2,1)S(1)}, bf16[48,384]{1,0:T(8,128)(2,1)S(1)}, u32[]{:S(2)}, u32[]{:S(2)}) collective-permute-start(bf16[48,384]{1,0:T(8,128)(2,1)S(1)} %reduce_sum.12), channel_id=1, source_target_pairs={{0,16},{8,24},{16,0},{24,8},{32,48},{40,56},{48,32},{56,40},{64,80... | collective-permute-start | bytes 110600 | tf_op jit(solution)/shard_map/ppermute | solution.py:236
  98.4 5.5 %collective-permute-start.8 = (bf16[48,384]{1,0:T(8,128)(2,1)S(1)}, bf16[48,384]{1,0:T(8,128)(2,1)S(1)}, u32[]{:S(2)}, u32[]{:S(2)}) collective-permute-start(bf16[48,384]{1,0:T(8,128)(2,1)S(1)} %reduce_sum.12), channel_id=1, source_target_pairs={{0,8},{8,16},{16,24},{24,0},{32,40},{40,48},{48,56},{56,32},{64,72... | collective-permute-start | bytes 110600 | tf_op jit(solution)/shard_map/ppermute | solution.py:236
  98.5 5.9 %collective-permute-start.9 = (bf16[48,384]{1,0:T(8,128)(2,1)S(1)}, bf16[48,384]{1,0:T(8,128)(2,1)S(1)}, u32[]{:S(2)}, u32[]{:S(2)}) collective-permute-start(bf16[48,384]{1,0:T(8,128)(2,1)S(1)} %reduce_sum.12), channel_id=1, source_target_pairs={{0,24},{8,0},{16,8},{24,16},{32,56},{40,32},{48,40},{56,48},{64,88... | collective-permute-start | bytes 110600 | tf_op jit(solution)/shard_map/ppermute | solution.py:236
  104.4 15.7 %collective-permute-start.10 = (bf16[48,384]{1,0:T(8,128)(2,1)S(1)}, bf16[48,384]{1,0:T(8,128)(2,1)S(1)}, u32[]{:S(2)}, u32[]{:S(2)}) collective-permute-start(bf16[48,384]{1,0:T(8,128)(2,1)S(1)} %add_convert_fusion.1), channel_id=1, source_target_pairs={{0,64},{8,72},{16,80},{24,88},{32,96},{40,104},{48,112},{56,120},{... | collective-permute-start | bytes 110600 | tf_op jit(solution)/shard_map/ppermute | solution.py:236
  109.8 10.4 %collective-permute-start.11 = (bf16[48,384]{1,0:T(8,128)(2,1)S(1)}, bf16[48,384]{1,0:T(8,128)(2,1)S(1)}, u32[]{:S(2)}, u32[]{:S(2)}) collective-permute-start(bf16[48,384]{1,0:T(8,128)(2,1)S(1)} %add_convert_fusion.1), channel_id=1, source_target_pairs={{0,32},{8,40},{16,48},{24,56},{32,64},{40,72},{48,80},{56,88},{64,... | collective-permute-start | bytes 110600 | tf_op jit(solution)/shard_map/ppermute | solution.py:236
  112.1 8.0 %collective-permute-start.12 = (bf16[48,384]{1,0:T(8,128)(2,1)S(1)}, bf16[48,384]{1,0:T(8,128)(2,1)S(1)}, u32[]{:S(2)}, u32[]{:S(2)}) collective-permute-start(bf16[48,384]{1,0:T(8,128)(2,1)S(1)} %add_convert_fusion.1), channel_id=1, source_target_pairs={{0,96},{8,104},{16,112},{24,120},{32,0},{40,8},{48,16},{56,24},{64... | collective-permute-start | bytes 110600 | tf_op jit(solution)/shard_map/ppermute | solution.py:236
  120.9 15.2 %all-to-all-start.4 = ((bf16[8,48,384]{2,1,0:T(8,128)(2,1)}), bf16[8,48,384]{2,1,0:T(8,128)(2,1)S(1)}, u32[]{:S(2)}, u32[]{:S(2)}) async-start(bf16[8,48,384]{2,1,0:T(8,128)(2,1)} %broadcast_in_dim.14), calls=%async_computation.4 | async-start | bytes 589824 | tf_op jit(solution)/shard_map/all_to_all | solution.py:216

commit v3 on v2

--- a/solution.py
+++ b/solution.py
@@ -16,7 +16,7 @@
 QUAD = 4
 SPAN = 512
 RING = 4
-CLOSE = 5
+CLOSE = 4
 NLON_BITS = 10
 MIB = 1 << 20
 
@@ -136,8 +136,8 @@
     )(lat, cells, weight, mask, source, own)
 
 
-def edge_kernel(rows, close_ref, far_ref, partial_ref, low_close_ref, low_far_ref, high_close_ref, high_far_ref, forced_ref):
-    lon_dev = low_close_ref.shape[0] // CLOSE
+def close_kernel(rows, close_ref, partial_ref, low_ref, high_ref, out_ref):
+    lon_dev = low_ref.shape[0] // CLOSE
     size, steps = QUAD * lon_dev, rows // QUAD
     for block in range(steps):
         below = block < steps // 2
@@ -145,28 +145,35 @@
         skip = max(0, QUAD * place - (REACH - CLOSE)) * lon_dev
         used = slice(skip, None) if below else slice(0, CLOSE * lon_dev - skip)
         span = slice(block * size, (block + 1) * size)
-        halo_ref = low_close_ref if below else high_close_ref
-        value = partial_ref[span, :] + across(close_ref[used, span], halo_ref[used, :])
-        if place == 0:
-            distant_ref = low_far_ref if below else high_far_ref
-            far_span = slice(0, size) if below else slice(size, 2 * size)
-            value = value + across(far_ref[:, far_span], distant_ref[...])
-        forced_ref[span, :] = value.astype(forced_ref.dtype)
-
-
-def edge_part(close, far, partial, low_close, low_far, high_close, high_far, rows):
-    targets, channels = partial.shape
+        halo_ref = low_ref if below else high_ref
+        out_ref[span, :] = partial_ref[span, :] + across(close_ref[used, span], halo_ref[used, :])
+
+
+def far_kernel(rows, far_ref, partial_ref, low_ref, high_ref, forced_ref):
+    size = far_ref.shape[1] // 2
+    last = partial_ref.shape[0] - size
+    forced_ref[size:last, :] = partial_ref[size:last, :].astype(forced_ref.dtype)
+    low = partial_ref[:size, :] + across(far_ref[:, :size], low_ref[...])
+    forced_ref[:size, :] = low.astype(forced_ref.dtype)
+    high = partial_ref[last:, :] + across(far_ref[:, size:], high_ref[...])
+    forced_ref[last:, :] = high.astype(forced_ref.dtype)
+
+
+def edge_call(kernel, dtype, cost, hot, partial, low, high, rows):
     vmem = pl.BlockSpec(memory_space=pltpu.VMEM)
     return pl.pallas_call(
-        functools.partial(edge_kernel, rows),
-        out_shape=jax.ShapeDtypeStruct((targets, channels), jnp.bfloat16),
-        in_specs=[vmem] * 7,
+        functools.partial(kernel, rows),
+        out_shape=jax.ShapeDtypeStruct(partial.shape, dtype),
+        in_specs=[vmem] * 4,
         out_specs=vmem,
         compiler_params=pltpu.CompilerParams(vmem_limit_bytes=24 * MIB),
-        cost_estimate=pl.CostEstimate(
-            flops=2 * targets * close.shape[0] * channels, bytes_accessed=10 * MIB, transcendentals=0
-        ),
-    )(close, far, partial, low_close, low_far, high_close, high_far)
+        cost_estimate=pl.CostEstimate(flops=cost, bytes_accessed=1 << 20, transcendentals=0),
+    )(hot, partial, low, high)
+
+
+def edge_part(close, far, partial, low_close, low_far, high_close, high_far, rows):
+    partial = edge_call(close_kernel, jnp.float32, 1 << 30, close, partial, low_close, high_close, rows)
+    return edge_call(far_kernel, jnp.bfloat16, 1 << 28, far, partial, low_far, high_far, rows)
 
 
 def spectral_kernel(scale, filter_ref, x_ref, cot_ref, weight_ref, out_ref, grad_ref):

time: 138 us -> 134 us (0.971)
  waiting for transfers between devices: 28.5 us -> 22.7 us
    ppermute x4, waiting for transfers between devices: 12.2 us -> 6.21 us  [send(): lax.ppermute(block, ('comp', 'lat'), route(pairs, lax.axis_size('lat'), s...]
    ppermute x6, starting transfers between devices: 11.7 us -> 13.7 us  [gather_sum(): parts.append(lax.ppermute(piece, 'lat', pairs).astype(jnp.float32))]
    unnamed x12, local copies, waits for them, and re-layouts: 0.04 us -> 1.53 us
    pallas_call x1 -> x2, Pallas kernels: 3.15 us -> 3.05 us  [edge_call(): pl.pallas_call(functools.partial(kernel, rows), out_shape=jax.ShapeDtypeS...]
  transfers between devices with their start and end apart: 16 -> 16, of which waited for: 6 -> 8; matrix products, arithmetic and copies ran while one was open for 3% -> 3% of each run, Pallas kernels for 10% -> 10%
where the time goes in v3:
time: 134 us; the launch traced here: 133 us
  starting transfers between devices  45 us (34%)
  blocking collectives  37.9 us (28%)
  waiting for transfers between devices  22.7 us (17%)
  Pallas kernels  20 us (15%)
  local copies, waits for them, and re-layouts  3.48 us (3%)
  other arithmetic  3.36 us (3%)
    all_to_all x2, blocking collectives, spread(): return lax.all_to_all(block, axis, split_axis=0, concat_axis=0, tiled=True)  37.9 us
    all_to_all x3, starting transfers between devices, spread(): return lax.all_to_all(block, axis, split_axis=0, concat_axis=0, tiled=True)  16.1 us
    ppermute x6, starting transfers between devices, gather_sum(): parts.append(lax.ppermute(piece, 'lat', pairs).astype(jnp.float32))  13.7 us
    pallas_call x1, Pallas kernels, near_part(): pl.pallas_call(near_kernel, out_shape=(jax.ShapeDtypeStruct((targets, cha...  10.9 us
    ppermute x6, waiting for transfers between devices, gather_sum(): parts.append(lax.ppermute(piece, 'lat', pairs).astype(jnp.float32))  9.17 us
    ppermute x4, starting transfers between devices, send(): lax.ppermute(block, ('comp', 'lat'), route(pairs, lax.axis_size('lat'), s...  8.78 us
    ppermute x4, waiting for transfers between devices, send(): lax.ppermute(block, ('comp', 'lat'), route(pairs, lax.axis_size('lat'), s...  6.21 us
    all_to_all x3, waiting for transfers between devices, spread(): return lax.all_to_all(block, axis, split_axis=0, concat_axis=0, tiled=True)  6.17 us
  transfers between devices with their start and end apart: 16, of which 8 were waited for; matrix products, arithmetic and copies ran while one was open for 3% of the time, Pallas kernels for 10%

profile of v3, /device:TPU:24, one launch (start us, length us, event | category | flops | bytes accessed | tf_op | source)
XLA Modules:
  0.0 133.3 jit_solution(626042983341681963)
XLA Ops:
  0.7 5.8 %all-to-all-start.1 = ((bf16[16,128,384]{2,1,0:T(8,128)(2,1)}), bf16[16,128,384]{2,1,0:T(8,128)(2,1)S(1)}, u32[]{:S(2)}, u32[]{:S(2)}) async-start(bf16[16,128,384]{2,1,0:T(8,128)(2,1)} %bitcast.45), calls=%async_computation.1 | async-start | bytes 3145728 | tf_op jit(solution)/shard_map/all_to_all | solution.py:223
  6.6 1.2 slice_bitcast_fusion
  7.8 2.1 %collective-permute-start.3 = (bf16[4,128,384]{2,1,0:T(8,128)(2,1)}, bf16[4,128,384]{2,1,0:T(8,128)(2,1)}, u32[]{:S(2)}, u32[]{:S(2)}) collective-permute-start(bf16[4,128,384]{2,1,0:T(8,128)(2,1)} %get-tuple-element.18), channel_id=1, source_target_pairs={{0,136},{8,144},{16,152},{32,168},{40,176},{48,184},{64,200},{72,2... | collective-permute-start | bytes 1179656 | tf_op jit(solution)/shard_map/ppermute | solution.py:291
  9.9 4.2 %collective-permute-start.5 = (bf16[4,128,384]{2,1,0:T(8,128)(2,1)}, bf16[4,128,384]{2,1,0:T(8,128)(2,1)}, u32[]{:S(2)}, u32[]{:S(2)}) collective-permute-start(bf16[4,128,384]{2,1,0:T(8,128)(2,1)} %get-tuple-element.19), channel_id=1, source_target_pairs={{8,128},{16,136},{24,144},{40,160},{48,168},{56,176},{72,192},{80,... | collective-permute-start | bytes 1179656 | tf_op jit(solution)/shard_map/ppermute | solution.py:292
  14.1 4.9 %collective-permute-start.1 = (bf16[4,128,384]{2,1,0:T(8,128)(2,1)}, bf16[4,128,384]{2,1,0:T(8,128)(2,1)S(1)}, u32[]{:S(2)}, u32[]{:S(2)}) collective-permute-start(bf16[4,128,384]{2,1,0:T(8,128)(2,1)} %get-tuple-element.29), channel_id=1, source_target_pairs={{0,136},{8,144},{16,152},{24,160},{32,168},{40,176},{48,184},{56,1... | collective-permute-start | bytes 1179656 | tf_op jit(solution)/shard_map/ppermute | solution.py:272
  19.0 1.9 %collective-permute-start.2 = (bf16[4,128,384]{2,1,0:T(8,128)(2,1)}, bf16[4,128,384]{2,1,0:T(8,128)(2,1)}, u32[]{:S(2)}, u32[]{:S(2)}) collective-permute-start(bf16[4,128,384]{2,1,0:T(8,128)(2,1)} %get-tuple-element.26), channel_id=1, source_target_pairs={{8,128},{16,136},{24,144},{32,152},{40,160},{48,168},{56,176},{64,... | collective-permute-start | bytes 1179656 | tf_op jit(solution)/shard_map/ppermute | solution.py:272
  21.8 1.0 collective-permute-done.5
  22.8 1.3 collective-permute-start.6
  24.1 0.7 copy-done.2
  24.9 0.8 copy-done.3
  25.6 10.9 %shard_map.86 = (f32[2048,384]{1,0:T(8,128)S(1)}, bf16[512,2048]{1,0:T(8,128)(2,1)S(1)}, bf16[512,1024]{1,0:T(8,128)(2,1)S(1)}) custom-call(s32[1]{0:T(128)} %bitcast.lat_ref, s32[4,16,128]{2,1,0:T(8,128)S(1)} %bitcast.42, f32[4,16,128]{2,1,0:T(8,128)S(1)} %bitcast.43, s32[16,128]{1,0:T(8,128)S(1)} %bitcast.44, bf16[2048,384]{1,0:T(8,128)(2,1)} %bitcast.7.source_ref, ...), custom_call_target="tpu_custom_call" | custom-call | flops 3221225472 | bytes 16777216 | tf_op jit(solution)/shard_map/pallas_call | solution.py:118
  36.6 6.2 %collective-permute-done.2 = bf16[4,128,384]{2,1,0:T(8,128)(2,1)} collective-permute-done((bf16[4,128,384]{2,1,0:T(8,128)(2,1)}, bf16[4,128,384]{2,1,0:T(8,128)(2,1)}, u32[]{:S(2)}, u32[]{:S(2)}) %collective-permute-start.2) | collective-permute-done | bytes 393248 | tf_op jit(solution)/shard_map/ppermute | solution.py:272
  42.8 2.3 %shard_map.87.partial_ref = f32[2048,384]{1,0:T(8,128)S(1)} custom-call(bf16[512,2048]{1,0:T(8,128)(2,1)S(1)} %get-tuple-element.16.close_ref, f32[2048,384]{1,0:T(8,128)S(1)} %get-tuple-element.17.partial_ref, bf16[512,384]{1,0:T(8,128)(2,1)S(1)} %bitcast.39, bf16[512,384]{1,0:T(8,128)(2,1)} %bitcast.12.high_ref), custom_call_target="tpu_custom_call" | custom-call | flops 1073741824 | bytes 1048576 | tf_op jit(solution)/shard_map/pallas_call | solution.py:164
  45.1 1.1 broadcast_select_fusion.1
  46.2 0.8 shard_map.88
  47.0 27.2 %all_to_all.25 = bf16[16,128,384]{2,1,0:T(8,128)(2,1)S(1)} all-to-all(bf16[16,128,384]{2,1,0:T(8,128)(2,1)S(1)} %bitcast.32), channel_id=1, replica_groups=mesh['comp'=2,'lat'=16,'lon'=8] {'lon'}, dimensions={0} | all-to-all | bytes 3145728 | tf_op jit(solution)/shard_map/all_to_all | solution.py:223
  74.3 6.1 %shard_map.89 = (bf16[8,2,128,384]{3,2,1,0:T(8,128)(2,1)}, bf16[384,384]{1,0:T(8,128)(2,1)S(1)}) custom-call(bf16[1024,1024]{1,0:T(8,128)(2,1)S(1)} %copy-done.5, bf16[8,2,128,384]{3,2,1,0:T(8,128)(2,1)S(1)} %bitcast.36, bf16[8,2,128,384]{3,2,1,0:T(8,128)(2,1)S(1)} %bitcast.35, bf16[384,384]{1,0:T(8,128)(2,1)S(1)} %bitcast.41), custom_call_target="tpu_custom_call" | custom-call | flops 2818572288 | bytes 8388608 | tf_op jit(solution)/shard_map/pallas_call | solution.py:205
  80.3 10.6 %all_to_all.26 = bf16[8,48,384]{2,1,0:T(8,128)(2,1)S(1)} all-to-all(bf16[8,48,384]{2,1,0:T(8,128)(2,1)S(1)} %bitcast.40), channel_id=1, replica_groups=mesh['comp'=2,'lat'=16,'lon'=8] {'lon'}, dimensions={0} | all-to-all | bytes 589824 | tf_op jit(solution)/shard_map/all_to_all | solution.py:223
  90.9 3.6 %all-to-all-start.3 = ((bf16[16,128,384]{2,1,0:T(8,128)(2,1)}), bf16[16,128,384]{2,1,0:T(8,128)(2,1)S(1)}, u32[]{:S(2)}, u32[]{:S(2)}) async-start(bf16[16,128,384]{2,1,0:T(8,128)(2,1)} %bitcast.20), calls=%async_computation.3 | async-start | bytes 3145728 | tf_op jit(solution)/shard_map/all_to_all | solution.py:223
  94.7 0.7 collective-permute-start.8
  95.4 1.4 %collective-permute-start.9 = (bf16[48,384]{1,0:T(8,128)(2,1)S(1)}, bf16[48,384]{1,0:T(8,128)(2,1)S(1)}, u32[]{:S(2)}, u32[]{:S(2)}) collective-permute-start(bf16[48,384]{1,0:T(8,128)(2,1)S(1)} %reduce_sum.12), channel_id=1, source_target_pairs={{0,24},{8,0},{16,8},{24,16},{32,56},{40,32},{48,40},{56,48},{64,88... | collective-permute-start | bytes 110600 | tf_op jit(solution)/shard_map/ppermute | solution.py:243
  96.8 3.3 %collective-permute-done.7 = bf16[48,384]{1,0:T(8,128)(2,1)S(1)} collective-permute-done((bf16[48,384]{1,0:T(8,128)(2,1)S(1)}, bf16[48,384]{1,0:T(8,128)(2,1)S(1)}, u32[]{:S(2)}, u32[]{:S(2)}) %collective-permute-start.7) | collective-permute-done | bytes 36896 | tf_op jit(solution)/shard_map/ppermute | solution.py:243
  100.7 7.4 %collective-permute-start.10 = (bf16[48,384]{1,0:T(8,128)(2,1)S(1)}, bf16[48,384]{1,0:T(8,128)(2,1)S(1)}, u32[]{:S(2)}, u32[]{:S(2)}) collective-permute-start(bf16[48,384]{1,0:T(8,128)(2,1)S(1)} %add_convert_fusion.1), channel_id=1, source_target_pairs={{0,64},{8,72},{16,80},{24,88},{32,96},{40,104},{48,112},{56,120},{... | collective-permute-start | bytes 110600 | tf_op jit(solution)/shard_map/ppermute | solution.py:243
  108.1 0.7 collective-permute-start.11
  108.8 3.4 %collective-permute-start.12 = (bf16[48,384]{1,0:T(8,128)(2,1)S(1)}, bf16[48,384]{1,0:T(8,128)(2,1)S(1)}, u32[]{:S(2)}, u32[]{:S(2)}) collective-permute-start(bf16[48,384]{1,0:T(8,128)(2,1)S(1)} %add_convert_fusion.1), channel_id=1, source_target_pairs={{0,96},{8,104},{16,112},{24,120},{32,0},{40,8},{48,16},{56,24},{64... | collective-permute-start | bytes 110600 | tf_op jit(solution)/shard_map/ppermute | solution.py:243
  112.3 2.8 %collective-permute-done.10 = bf16[48,384]{1,0:T(8,128)(2,1)S(1)} collective-permute-done((bf16[48,384]{1,0:T(8,128)(2,1)S(1)}, bf16[48,384]{1,0:T(8,128)(2,1)S(1)}, u32[]{:S(2)}, u32[]{:S(2)}) %collective-permute-start.10) | collective-permute-done | bytes 36896 | tf_op jit(solution)/shard_map/ppermute | solution.py:243
  115.0 2.5 %collective-permute-done.11 = bf16[48,384]{1,0:T(8,128)(2,1)S(1)} collective-permute-done((bf16[48,384]{1,0:T(8,128)(2,1)S(1)}, bf16[48,384]{1,0:T(8,128)(2,1)S(1)}, u32[]{:S(2)}, u32[]{:S(2)}) %collective-permute-start.11) | collective-permute-done | bytes 36896 | tf_op jit(solution)/shard_map/ppermute | solution.py:243
  117.6 0.7 broadcast_in_dim.14
  118.3 6.7 %all-to-all-start.4 = ((bf16[8,48,384]{2,1,0:T(8,128)(2,1)}), bf16[8,48,384]{2,1,0:T(8,128)(2,1)S(1)}, u32[]{:S(2)}, u32[]{:S(2)}) async-start(bf16[8,48,384]{2,1,0:T(8,128)(2,1)} %broadcast_in_dim.14), calls=%async_computation.4 | async-start | bytes 589824 | tf_op jit(solution)/shard_map/all_to_all | solution.py:223
  125.0 1.3 select_bitcast_fusion
  126.3 6.2 %all-to-all-done.4 = bf16[8,48,384]{2,1,0:T(8,128)(2,1)S(1)} async-done(((bf16[8,48,384]{2,1,0:T(8,128)(2,1)}), bf16[8,48,384]{2,1,0:T(8,128)(2,1)S(1)}, u32[]{:S(2)}, u32[]{:S(2)}) %all-to-all-start.4) | async-done | bytes 294944 | tf_op jit(solution)/shard_map/all_to_all | solution.py:223
  132.4 0.9 bitcast_convert_fusion
  (27 shorter events, 1.8 us)
Async XLA Ops:
  0.6 7.1 %collective-permute-start = (bf16[16,128,384]{2,1,0:T(8,128)(2,1)}, bf16[16,128,384]{2,1,0:T(8,128)(2,1)}, u32[]{:S(2)}, u32[]{:S(2)}) collective-permute-start(bf16[16,128,384]{2,1,0:T(8,128)(2,1)} %bitcast.33), channel_id=1, source_target_pairs={{0,128},{128,0},{1,129},{129,1},{2,130},{130,2},{3,131},{131,3},{4... | collective-permute-start | bytes 4718600 | tf_op jit(solution)/shard_map/ppermute | solution.py:309
  0.7 5.8 %copy-start = (bf16[1,16,128,384]{3,2,1,0:T(8,128)(2,1)S(1)}, bf16[1,16,128,384]{3,2,1,0:T(8,128)(2,1)}, u32[]{:S(2)}) copy-start(bf16[1,16,128,384]{3,2,1,0:T(8,128)(2,1)} %param.7) | copy-start | bytes 4718596
  0.7 46.2 %all-to-all-start.1 = ((bf16[16,128,384]{2,1,0:T(8,128)(2,1)}), bf16[16,128,384]{2,1,0:T(8,128)(2,1)S(1)}, u32[]{:S(2)}, u32[]{:S(2)}) async-start(bf16[16,128,384]{2,1,0:T(8,128)(2,1)} %bitcast.45), calls=%async_computation.1 | async-start | bytes 3145728 | tf_op jit(solution)/shard_map/all_to_all | solution.py:223
  6.5 17.6 %copy-start.4 = (s32[1,16,128]{2,1,0:T(8,128)S(1)}, s32[1,16,128]{2,1,0:T(8,128)}, u32[]{:S(2)}) copy-start(s32[1,16,128]{2,1,0:T(8,128)} %param.10) | copy-start | bytes 24580
  7.8 13.3 %collective-permute-start.3 = (bf16[4,128,384]{2,1,0:T(8,128)(2,1)}, bf16[4,128,384]{2,1,0:T(8,128)(2,1)}, u32[]{:S(2)}, u32[]{:S(2)}) collective-permute-start(bf16[4,128,384]{2,1,0:T(8,128)(2,1)} %get-tuple-element.18), channel_id=1, source_target_pairs={{0,136},{8,144},{16,152},{32,168},{40,176},{48,184},{64,200},{72,2... | collective-permute-start | bytes 1179656 | tf_op jit(solution)/shard_map/ppermute | solution.py:291
  9.9 12.9 %collective-permute-start.5 = (bf16[4,128,384]{2,1,0:T(8,128)(2,1)}, bf16[4,128,384]{2,1,0:T(8,128)(2,1)}, u32[]{:S(2)}, u32[]{:S(2)}) collective-permute-start(bf16[4,128,384]{2,1,0:T(8,128)(2,1)} %get-tuple-element.19), channel_id=1, source_target_pairs={{8,128},{16,136},{24,144},{40,160},{48,168},{56,176},{72,192},{80,... | collective-permute-start | bytes 1179656 | tf_op jit(solution)/shard_map/ppermute | solution.py:292
  14.1 22.5 %collective-permute-start.1 = (bf16[4,128,384]{2,1,0:T(8,128)(2,1)}, bf16[4,128,384]{2,1,0:T(8,128)(2,1)S(1)}, u32[]{:S(2)}, u32[]{:S(2)}) collective-permute-start(bf16[4,128,384]{2,1,0:T(8,128)(2,1)} %get-tuple-element.29), channel_id=1, source_target_pairs={{0,136},{8,144},{16,152},{24,160},{32,168},{40,176},{48,184},{56,1... | collective-permute-start | bytes 1179656 | tf_op jit(solution)/shard_map/ppermute | solution.py:272
  19.0 23.8 %collective-permute-start.2 = (bf16[4,128,384]{2,1,0:T(8,128)(2,1)}, bf16[4,128,384]{2,1,0:T(8,128)(2,1)}, u32[]{:S(2)}, u32[]{:S(2)}) collective-permute-start(bf16[4,128,384]{2,1,0:T(8,128)(2,1)} %get-tuple-element.26), channel_id=1, source_target_pairs={{8,128},{16,136},{24,144},{32,152},{40,160},{48,168},{56,176},{64,... | collective-permute-start | bytes 1179656 | tf_op jit(solution)/shard_map/ppermute | solution.py:272
  21.1 24.0 %collective-permute-start.4 = (bf16[4,128,384]{2,1,0:T(8,128)(2,1)}, bf16[4,128,384]{2,1,0:T(8,128)(2,1)S(1)}, u32[]{:S(2)}, u32[]{:S(2)}) collective-permute-start(bf16[4,128,384]{2,1,0:T(8,128)(2,1)} %collective-permute-done.3), channel_id=1, source_target_pairs={{0,160},{32,192},{64,224},{128,32},{160,64},{192,96},{1,161},{33,1... | collective-permute-start | bytes 1179656 | tf_op jit(solution)/shard_map/ppermute | solution.py:272
  22.8 23.3 %collective-permute-start.6 = (bf16[4,128,384]{2,1,0:T(8,128)(2,1)}, bf16[4,128,384]{2,1,0:T(8,128)(2,1)S(1)}, u32[]{:S(2)}, u32[]{:S(2)}) collective-permute-start(bf16[4,128,384]{2,1,0:T(8,128)(2,1)} %collective-permute-done.5), channel_id=1, source_target_pairs={{56,152},{88,184},{120,216},{184,24},{216,56},{248,88},{57,153},{8... | collective-permute-start | bytes 1179656 | tf_op jit(solution)/shard_map/ppermute | solution.py:272
  24.1 0.8 copy-start.2
  24.9 0.8 copy-start.3
  47.0 27.3 %copy-start.1 = (bf16[1,384,384]{2,1,0:T(8,128)(2,1)S(1)}, bf16[1,384,384]{2,1,0:T(8,128)(2,1)}, u32[]{:S(2)}) copy-start(bf16[1,384,384]{2,1,0:T(8,128)(2,1)} %param.11) | copy-start | bytes 884740
  47.0 27.3 %copy-start.5 = (bf16[1024,1024]{1,0:T(8,128)(2,1)S(1)}, bf16[1024,1024]{1,0:T(8,128)(2,1)}, u32[]{:S(2)}) copy-start(bf16[1024,1024]{1,0:T(8,128)(2,1)} %constant.29.clone.filter_ref) | copy-start | bytes 6291460
  90.9 26.6 %all-to-all-start.3 = ((bf16[16,128,384]{2,1,0:T(8,128)(2,1)}), bf16[16,128,384]{2,1,0:T(8,128)(2,1)S(1)}, u32[]{:S(2)}, u32[]{:S(2)}) async-start(bf16[16,128,384]{2,1,0:T(8,128)(2,1)} %bitcast.20), calls=%async_computation.3 | async-start | bytes 3145728 | tf_op jit(solution)/shard_map/all_to_all | solution.py:223
  94.6 5.5 %collective-permute-start.7 = (bf16[48,384]{1,0:T(8,128)(2,1)S(1)}, bf16[48,384]{1,0:T(8,128)(2,1)S(1)}, u32[]{:S(2)}, u32[]{:S(2)}) collective-permute-start(bf16[48,384]{1,0:T(8,128)(2,1)S(1)} %reduce_sum.12), channel_id=1, source_target_pairs={{0,16},{8,24},{16,0},{24,8},{32,48},{40,56},{48,32},{56,40},{64,80... | collective-permute-start | bytes 110600 | tf_op jit(solution)/shard_map/ppermute | solution.py:243
  94.7 5.5 %collective-permute-start.8 = (bf16[48,384]{1,0:T(8,128)(2,1)S(1)}, bf16[48,384]{1,0:T(8,128)(2,1)S(1)}, u32[]{:S(2)}, u32[]{:S(2)}) collective-permute-start(bf16[48,384]{1,0:T(8,128)(2,1)S(1)} %reduce_sum.12), channel_id=1, source_target_pairs={{0,8},{8,16},{16,24},{24,0},{32,40},{40,48},{48,56},{56,32},{64,72... | collective-permute-start | bytes 110600 | tf_op jit(solution)/shard_map/ppermute | solution.py:243
  95.4 5.3 %collective-permute-start.9 = (bf16[48,384]{1,0:T(8,128)(2,1)S(1)}, bf16[48,384]{1,0:T(8,128)(2,1)S(1)}, u32[]{:S(2)}, u32[]{:S(2)}) collective-permute-start(bf16[48,384]{1,0:T(8,128)(2,1)S(1)} %reduce_sum.12), channel_id=1, source_target_pairs={{0,24},{8,0},{16,8},{24,16},{32,56},{40,32},{48,40},{56,48},{64,88... | collective-permute-start | bytes 110600 | tf_op jit(solution)/shard_map/ppermute | solution.py:243
  100.7 14.3 %collective-permute-start.10 = (bf16[48,384]{1,0:T(8,128)(2,1)S(1)}, bf16[48,384]{1,0:T(8,128)(2,1)S(1)}, u32[]{:S(2)}, u32[]{:S(2)}) collective-permute-start(bf16[48,384]{1,0:T(8,128)(2,1)S(1)} %add_convert_fusion.1), channel_id=1, source_target_pairs={{0,64},{8,72},{16,80},{24,88},{32,96},{40,104},{48,112},{56,120},{... | collective-permute-start | bytes 110600 | tf_op jit(solution)/shard_map/ppermute | solution.py:243
  108.1 9.4 %collective-permute-start.11 = (bf16[48,384]{1,0:T(8,128)(2,1)S(1)}, bf16[48,384]{1,0:T(8,128)(2,1)S(1)}, u32[]{:S(2)}, u32[]{:S(2)}) collective-permute-start(bf16[48,384]{1,0:T(8,128)(2,1)S(1)} %add_convert_fusion.1), channel_id=1, source_target_pairs={{0,32},{8,40},{16,48},{24,56},{32,64},{40,72},{48,80},{56,88},{64,... | collective-permute-start | bytes 110600 | tf_op jit(solution)/shard_map/ppermute | solution.py:243
  108.8 8.7 %collective-permute-start.12 = (bf16[48,384]{1,0:T(8,128)(2,1)S(1)}, bf16[48,384]{1,0:T(8,128)(2,1)S(1)}, u32[]{:S(2)}, u32[]{:S(2)}) collective-permute-start(bf16[48,384]{1,0:T(8,128)(2,1)S(1)} %add_convert_fusion.1), channel_id=1, source_target_pairs={{0,96},{8,104},{16,112},{24,120},{32,0},{40,8},{48,16},{56,24},{64... | collective-permute-start | bytes 110600 | tf_op jit(solution)/shard_map/ppermute | solution.py:243
  118.3 14.2 %all-to-all-start.4 = ((bf16[8,48,384]{2,1,0:T(8,128)(2,1)}), bf16[8,48,384]{2,1,0:T(8,128)(2,1)S(1)}, u32[]{:S(2)}, u32[]{:S(2)}) async-start(bf16[8,48,384]{2,1,0:T(8,128)(2,1)} %broadcast_in_dim.14), calls=%async_computation.4 | async-start | bytes 589824 | tf_op jit(solution)/shard_map/all_to_all | solution.py:223
